TPU v7x, 128 devices: a whole 4x4x4 slice. The times are simulated.
128 devices in a mesh: lag: 16 (over y, x_hi, core), src: 8 (over z, x_lo).
Axes of the slice: x: 4 (x_hi: 2, x_lo: 2; x = x_hi * 2 + x_lo), y: 4, z: 4, core: 2. Of those that a mesh axis runs over, the one named last changes fastest.
Arguments:
- reflection: bfloat16 [1024, 16, 2048], P(None, 'src', 'lag'), may hold values from -0.046875 to 0.046875
- focus_plus: bfloat16 [16, 8, 2048], P('src', None, 'lag'), may hold values from -6 to 6
- focus_start: bfloat16 [16, 8, 2048], P('src', None, 'lag'), may hold values from -6 to 6
- onset_receiver: int32 [1024, 8], replicated, may hold values from 128 to 1024, as said below
- onset_source: int32 [16, 8], P('src'), may hold values from 128 to 1024, as said below
Outputs:
- focus_minus: bfloat16 [1024, 8, 2048], P('src', None, 'lag')
- focus_next: float32 [16, 8, 2048], P('src', None, 'lag')
Inputs may be any that keep to these rules, and one draw needn't show every extreme that they name: `onset_receiver`: onset of the direct arrival in samples from the middle of the time axis. `onset_source`: onset of the direct arrival in samples from the middle of the time axis.
All inputs are finite; a program needn't handle non-finite values.
Results may differ from a plain program's by a relative error of at most 0.012.
Values may be sent and summed in bfloat16 or wider, within the bound.
A program may use at most 128 MiB of HBM per device.

v0:
```python
import jax
import jax.numpy as jnp
from jax import lax
from jax.sharding import PartitionSpec as P


def shifted(array, axis, by):
    devices = lax.axis_size(axis)
    pairs = [(i, i + by) for i in range(devices) if 0 <= i + by < devices]
    return lax.ppermute(array, axis, pairs)


def swapped(value, axis, apart):
    mask = 2**apart
    pairs = [(source, source ^ mask) for source in range(lax.axis_size(axis))]
    return lax.ppermute(value, axis, pairs)


def causal_window_mask(onset_index, sample_index, centre):
    lower_edge = centre - onset_index[..., None]
    upper_edge = centre - 1 + onset_index[..., None]
    inside = (sample_index >= lower_edge) & (sample_index <= upper_edge)
    return jnp.where(inside, 1.0, 0.0).astype(jnp.float32)


def toeplitz(focus_pair, lag_len):
    source_count, focal_count, _ = focus_pair.shape
    rolled = jnp.concatenate([focus_pair[:, :, lag_len:], focus_pair[:, :, :lag_len]], axis=2)
    tiled_rows = jnp.broadcast_to(
        rolled[:, :, None, :], (source_count, focal_count, lag_len, 2 * lag_len)
    )
    flat_rows = tiled_rows.reshape(source_count, focal_count, 2 * lag_len * lag_len)
    flat_rows = flat_rows[:, :, : lag_len * (2 * lag_len - 1)]
    return flat_rows.reshape(source_count, focal_count, lag_len, 2 * lag_len - 1)[:, :, :, :lag_len]


def shear_sum(matrix_product, lag_len):
    source_count, focal_count = (matrix_product.shape[0], matrix_product.shape[1])
    padded = jnp.concatenate([jnp.zeros_like(matrix_product), matrix_product], axis=3)
    flat_rows = padded.reshape(source_count, focal_count, 2 * lag_len * lag_len)
    flat_rows = jnp.pad(flat_rows, ((0, 0), (0, 0), (0, lag_len)))
    skewed = flat_rows.reshape(source_count, focal_count, lag_len, 2 * lag_len + 1)[
        :, :, :, : 2 * lag_len
    ]
    return jnp.sum(skewed, axis=2)


def forward_term(block_of_lags, reversal_index, focus_padded, lag_len):
    focus_pair = lax.dynamic_slice_in_dim(
        focus_padded, reversal_index * lag_len, 2 * lag_len, axis=2
    )
    reflection_matrix = toeplitz(focus_pair, lag_len)
    return jnp.einsum(
        "kne,njea->kja", block_of_lags, reflection_matrix, preferred_element_type=jnp.float32
    )


def backward_term(block_of_lags, reversal_index, full_minus_field, lag_len, running_sum):
    matrix_product = jnp.einsum(
        "exq,enc->xnqc", block_of_lags, full_minus_field, preferred_element_type=jnp.float32
    )
    sheared = shear_sum(matrix_product, lag_len)
    running_sum = running_sum.at[reversal_index].add(sheared[:, :, :lag_len])
    return running_sum.at[reversal_index + 1].add(sheared[:, :, lag_len:])


def walk_chain(reflection, update, initial):
    lane_count = lax.axis_size("lag")

    def advance(reversal_index, loop_state):
        block_of_lags, running = loop_state
        running = update(block_of_lags, reversal_index, running)
        moved_block = shifted(block_of_lags, "lag", 1)
        return (moved_block, running)

    _, running = lax.fori_loop(0, lane_count, advance, (reflection, initial))
    return running


def body(reflection, focus_plus, focus_start, onset_receiver, onset_source):
    receivers_all, _, lag_len = reflection.shape
    focal_count = focus_plus.shape[1]
    lane_count = lax.axis_size("lag")
    groups = lax.axis_size("src")
    rows_per_share = receivers_all // groups
    centre = lane_count * lag_len // 2
    sample_index = lax.axis_index("lag") * lag_len + jnp.arange(lag_len, dtype=jnp.int32)
    row_count, source_count = (reflection.shape[0], reflection.shape[1])
    focus_all = lax.all_gather(focus_plus, "lag", axis=2, tiled=True)
    focus_padded = jnp.concatenate([jnp.zeros_like(focus_plus), focus_all], axis=2)

    def forward_update(block_of_lags, reversal_index, running):
        return running + forward_term(block_of_lags, reversal_index, focus_padded, lag_len)

    upgoing_init = jnp.zeros((row_count, focal_count, lag_len), jnp.float32)
    upgoing_part = walk_chain(reflection, forward_update, upgoing_init)
    onset_share = lax.dynamic_slice_in_dim(
        onset_receiver, lax.axis_index("src") * rows_per_share, rows_per_share, 0
    )
    upgoing_share = lax.psum_scatter(upgoing_part, "src", scatter_dimension=0, tiled=True)
    focus_minus = (causal_window_mask(onset_share, sample_index, centre) * upgoing_share).astype(
        jnp.bfloat16
    )
    full_minus_field = lax.all_gather(focus_minus, "src", axis=0, tiled=True)

    def backward_update(block_of_lags, reversal_index, running):
        return backward_term(block_of_lags, reversal_index, full_minus_field, lag_len, running)

    backward_init = jnp.zeros((lane_count + 1, source_count, focal_count, lag_len), jnp.float32)
    correlated_result = walk_chain(reflection, backward_update, backward_init)
    blocks = correlated_result[1:]
    own_part = lax.psum_scatter(
        blocks.astype(jnp.bfloat16), "lag", scatter_dimension=0, tiled=True
    ).astype(jnp.float32)[0]
    for bit_index in range(lane_count.bit_length() - 1):
        own_part = swapped(own_part, "lag", bit_index)
    source_window = causal_window_mask(onset_source, sample_index, centre)
    focus_next = focus_start.astype(jnp.float32) + source_window * own_part[:, :, ::-1]
    return (focus_minus, focus_next)


def solution(mesh):
    return jax.shard_map(
        body,
        mesh=mesh,
        in_specs=(
            P(None, "src", "lag"),
            P("src", None, "lag"),
            P("src", None, "lag"),
            P(),
            P("src", None),
        ),
        out_specs=(P("src", None, "lag"), P("src", None, "lag")),
        check_vma=False,
    )
```

profile of v0, /device:TPU:1, one launch (start us, length us, event | category | flops | bytes accessed | tf_op | source)
XLA Modules:
  0.0 767.1 jit_solution(16865161993226954347)
XLA Ops:
  10.2 26.2 %all_gather.6 = bf16[2,8,2048]{2,1,0:T(8,128)(2,1)S(1)} all-gather(bf16[2,8,128]{2,1,0:T(8,128)(2,1)} %param.14), channel_id=1, replica_groups=mesh['lag'=16,'src'=8] {'lag'}, dimensions={2}, use_global_device_ids=true | all-gather | bytes 69632 | tf_op jit(solution)/shard_map/all_gather | solution.py:89
  36.4 201.7 %while.36 = (s32[]{:T(128)}, bf16[1024,2,128]{2,0,1:T(8,128)(2,1)S(1)}, f32[1024,8,128]{0,2,1:T(8,128)}, bf16[2,8,2176]{2,1,0:T(8,128)(2,1)S(1)}, s32[]{:T(128)}, /*index=5*/s32[]{:T(128)}, s32[]{:T(128)}, s32[]{:T(128)}, s32[]{}) while((s32[]{:T(128)}, bf16[1024,2,128]{2,0,1:T(8,128)(2,1)S(1)}, f32[1024,8,128]{0,2,1:T(8,128)}, ...), condition=%wide.region_1.0_spmd.clone, body=%wide.region_0.0_spmd.clone.sunk | while | flops 538984448 | bytes 17850576 | solution.py:76
  44.7 5.7 collective-permute-start.1
  54.0 4.9 bitcast_add_fusion.2
  66.0 4.9 bitcast_add_fusion.2
  78.1 4.9 bitcast_add_fusion.2
  83.0 4.2 collective-permute-start.1
  90.8 4.9 bitcast_add_fusion.2
  95.8 4.4 collective-permute-start.1
  103.8 4.9 bitcast_add_fusion.2
  108.7 4.4 collective-permute-start.1
  116.7 4.9 bitcast_add_fusion.2
  121.7 4.4 collective-permute-start.1
  129.7 4.9 bitcast_add_fusion.2
  134.6 4.4 collective-permute-start.1
  142.6 4.9 bitcast_add_fusion.2
  147.5 4.4 collective-permute-start.1
  155.5 4.9 bitcast_add_fusion.2
  160.5 4.4 collective-permute-start.1
  168.5 4.9 bitcast_add_fusion.2
  173.4 4.4 collective-permute-start.1
  181.4 4.9 bitcast_add_fusion.2
  186.4 4.4 collective-permute-start.1
  194.4 4.9 bitcast_add_fusion.2
  199.3 4.4 collective-permute-start.1
  207.3 4.9 bitcast_add_fusion.2
  212.3 4.4 collective-permute-start.1
  220.2 4.9 bitcast_add_fusion.2
  225.2 4.4 collective-permute-start.1
  233.2 4.9 bitcast_add_fusion.2
  238.1 5.4 copy.26
  244.5 92.5 %reduce-scatter.3.cloned.1.call-done = f32[128,8,128]{2,1,0:T(8,128)} async-done(((f32[1024,8,128]{2,1,0:T(8,128)}), f32[128,8,128]{2,1,0:T(8,128)}) %reduce-scatter.3.cloned.1.call-update) | async-done | bytes 524304 | tf_op jit(solution)/shard_map/reduce_scatter | solution.py:100
  339.2 52.2 %all-gather.2.cloned.1.call-done = bf16[1024,8,128]{2,1,0:T(8,128)(2,1)} async-done(((bf16[128,8,128]{2,1,0:T(8,128)(2,1)}), bf16[1024,8,128]{2,1,0:T(8,128)(2,1)}) %all-gather.2.cloned.1.call-update) | async-done | bytes 2097168 | tf_op jit(solution)/shard_map/all_gather | solution.py:104
  391.4 4.1 copy.28
  395.6 293.1 %while.35 = (s32[]{:T(128)}, bf16[1024,2,128]{2,0,1:T(8,128)(2,1)}, f32[17,2,8,128]{3,2,1,0:T(8,128)S(1)}, bf16[1024,8,128]{0,2,1:T(8,128)(2,1)}, s32[]{:T(128)}...) while((s32[]{:T(128)}, bf16[1024,2,128]{2,0,1:T(8,128)(2,1)}, ...), condition=%wide.region_7.8_spmd, body=%wide.region_3.7_spmd.sunk | while | flops 537399360 | bytes 26829028 | solution.py:76
  397.5 5.1 collective-permute-start
  410.1 3.7 reshape.209
  427.4 3.7 reshape.209
  435.2 3.8 collective-permute-start
  463.8 3.7 reshape.209
  471.6 4.7 collective-permute-start
  483.8 3.7 reshape.209
  501.1 3.7 reshape.209
  508.9 3.8 collective-permute-start
  545.3 4.7 collective-permute-start
  610.9 3.7 reshape.209
  618.7 4.7 collective-permute-start
  689.4 55.9 %reduce-scatter.5.cloned.1.call-done = bf16[1,2,8,128]{3,2,1,0:T(8,128)(2,1)} async-done(((bf16[16,2,8,128]{3,2,1,0:T(8,128)(2,1)}), bf16[1,2,8,128]{3,2,1,0:T(8,128)(2,1)}) %reduce-scatter.5.cloned.1.call-update) | async-done | bytes 4112 | tf_op jit(solution)/shard_map/reduce_scatter | solution.py:112
  (347 shorter events, 333.3 us)
Async XLA Ops:
  7.2 329.9 %reduce-scatter.3.cloned.1.call-start = ((), (), s32[]{:S(2)}) async-start(), calls=%async_computation.2 | async-start | bytes 4718592 | tf_op jit(solution)/shard_map/reduce_scatter | solution.py:100
  36.5 8.2 %collective-permute-start.1 = (bf16[1024,2,128]{2,0,1:T(8,128)(2,1)S(1)}, bf16[1024,2,128]{2,0,1:T(8,128)(2,1)S(1)}, u32[]{:S(2)}, u32[]{:S(2)}) collective-permute-start(bf16[1024,2,128]{2,0,1:T(8,128)(2,1)S(1)} %copy.41), channel_id=1, source_target_pairs={{0,8},{8,16},{16,24},{24,32},{32,40},{40,48},{48,56},{56,64},{64,7... | collective-permute-start | bytes 1572872 | tf_op jit(solution)/shard_map/while/body/eval_jaxpr/ppermute | solution.py:10
  44.7 14.2 %collective-permute-start.1 = (bf16[1024,2,128]{2,0,1:T(8,128)(2,1)S(1)}, bf16[1024,2,128]{2,0,1:T(8,128)(2,1)S(1)}, u32[]{:S(2)}, u32[]{:S(2)}) collective-permute-start(bf16[1024,2,128]{2,0,1:T(8,128)(2,1)S(1)} %copy.41), channel_id=1, source_target_pairs={{0,8},{8,16},{16,24},{24,32},{32,40},{40,48},{48,56},{56,64},{64,7... | collective-permute-start | bytes 1572872 | tf_op jit(solution)/shard_map/while/body/eval_jaxpr/ppermute | solution.py:10
  58.9 12.0 %collective-permute-start.1 = (bf16[1024,2,128]{2,0,1:T(8,128)(2,1)S(1)}, bf16[1024,2,128]{2,0,1:T(8,128)(2,1)S(1)}, u32[]{:S(2)}, u32[]{:S(2)}) collective-permute-start(bf16[1024,2,128]{2,0,1:T(8,128)(2,1)S(1)} %copy.41), channel_id=1, source_target_pairs={{0,8},{8,16},{16,24},{24,32},{32,40},{40,48},{48,56},{56,64},{64,7... | collective-permute-start | bytes 1572872 | tf_op jit(solution)/shard_map/while/body/eval_jaxpr/ppermute | solution.py:10
  71.0 12.0 %collective-permute-start.1 = (bf16[1024,2,128]{2,0,1:T(8,128)(2,1)S(1)}, bf16[1024,2,128]{2,0,1:T(8,128)(2,1)S(1)}, u32[]{:S(2)}, u32[]{:S(2)}) collective-permute-start(bf16[1024,2,128]{2,0,1:T(8,128)(2,1)S(1)} %copy.41), channel_id=1, source_target_pairs={{0,8},{8,16},{16,24},{24,32},{32,40},{40,48},{48,56},{56,64},{64,7... | collective-permute-start | bytes 1572872 | tf_op jit(solution)/shard_map/while/body/eval_jaxpr/ppermute | solution.py:10
  83.0 12.7 %collective-permute-start.1 = (bf16[1024,2,128]{2,0,1:T(8,128)(2,1)S(1)}, bf16[1024,2,128]{2,0,1:T(8,128)(2,1)S(1)}, u32[]{:S(2)}, u32[]{:S(2)}) collective-permute-start(bf16[1024,2,128]{2,0,1:T(8,128)(2,1)S(1)} %copy.41), channel_id=1, source_target_pairs={{0,8},{8,16},{16,24},{24,32},{32,40},{40,48},{48,56},{56,64},{64,7... | collective-permute-start | bytes 1572872 | tf_op jit(solution)/shard_map/while/body/eval_jaxpr/ppermute | solution.py:10
  95.8 12.9 %collective-permute-start.1 = (bf16[1024,2,128]{2,0,1:T(8,128)(2,1)S(1)}, bf16[1024,2,128]{2,0,1:T(8,128)(2,1)S(1)}, u32[]{:S(2)}, u32[]{:S(2)}) collective-permute-start(bf16[1024,2,128]{2,0,1:T(8,128)(2,1)S(1)} %copy.41), channel_id=1, source_target_pairs={{0,8},{8,16},{16,24},{24,32},{32,40},{40,48},{48,56},{56,64},{64,7... | collective-permute-start | bytes 1572872 | tf_op jit(solution)/shard_map/while/body/eval_jaxpr/ppermute | solution.py:10
  108.7 12.9 %collective-permute-start.1 = (bf16[1024,2,128]{2,0,1:T(8,128)(2,1)S(1)}, bf16[1024,2,128]{2,0,1:T(8,128)(2,1)S(1)}, u32[]{:S(2)}, u32[]{:S(2)}) collective-permute-start(bf16[1024,2,128]{2,0,1:T(8,128)(2,1)S(1)} %copy.41), channel_id=1, source_target_pairs={{0,8},{8,16},{16,24},{24,32},{32,40},{40,48},{48,56},{56,64},{64,7... | collective-permute-start | bytes 1572872 | tf_op jit(solution)/shard_map/while/body/eval_jaxpr/ppermute | solution.py:10
  121.7 12.9 %collective-permute-start.1 = (bf16[1024,2,128]{2,0,1:T(8,128)(2,1)S(1)}, bf16[1024,2,128]{2,0,1:T(8,128)(2,1)S(1)}, u32[]{:S(2)}, u32[]{:S(2)}) collective-permute-start(bf16[1024,2,128]{2,0,1:T(8,128)(2,1)S(1)} %copy.41), channel_id=1, source_target_pairs={{0,8},{8,16},{16,24},{24,32},{32,40},{40,48},{48,56},{56,64},{64,7... | collective-permute-start | bytes 1572872 | tf_op jit(solution)/shard_map/while/body/eval_jaxpr/ppermute | solution.py:10
  134.6 12.9 %collective-permute-start.1 = (bf16[1024,2,128]{2,0,1:T(8,128)(2,1)S(1)}, bf16[1024,2,128]{2,0,1:T(8,128)(2,1)S(1)}, u32[]{:S(2)}, u32[]{:S(2)}) collective-permute-start(bf16[1024,2,128]{2,0,1:T(8,128)(2,1)S(1)} %copy.41), channel_id=1, source_target_pairs={{0,8},{8,16},{16,24},{24,32},{32,40},{40,48},{48,56},{56,64},{64,7... | collective-permute-start | bytes 1572872 | tf_op jit(solution)/shard_map/while/body/eval_jaxpr/ppermute | solution.py:10
  147.5 12.9 %collective-permute-start.1 = (bf16[1024,2,128]{2,0,1:T(8,128)(2,1)S(1)}, bf16[1024,2,128]{2,0,1:T(8,128)(2,1)S(1)}, u32[]{:S(2)}, u32[]{:S(2)}) collective-permute-start(bf16[1024,2,128]{2,0,1:T(8,128)(2,1)S(1)} %copy.41), channel_id=1, source_target_pairs={{0,8},{8,16},{16,24},{24,32},{32,40},{40,48},{48,56},{56,64},{64,7... | collective-permute-start | bytes 1572872 | tf_op jit(solution)/shard_map/while/body/eval_jaxpr/ppermute | solution.py:10
  160.5 12.9 %collective-permute-start.1 = (bf16[1024,2,128]{2,0,1:T(8,128)(2,1)S(1)}, bf16[1024,2,128]{2,0,1:T(8,128)(2,1)S(1)}, u32[]{:S(2)}, u32[]{:S(2)}) collective-permute-start(bf16[1024,2,128]{2,0,1:T(8,128)(2,1)S(1)} %copy.41), channel_id=1, source_target_pairs={{0,8},{8,16},{16,24},{24,32},{32,40},{40,48},{48,56},{56,64},{64,7... | collective-permute-start | bytes 1572872 | tf_op jit(solution)/shard_map/while/body/eval_jaxpr/ppermute | solution.py:10
  173.4 12.9 %collective-permute-start.1 = (bf16[1024,2,128]{2,0,1:T(8,128)(2,1)S(1)}, bf16[1024,2,128]{2,0,1:T(8,128)(2,1)S(1)}, u32[]{:S(2)}, u32[]{:S(2)}) collective-permute-start(bf16[1024,2,128]{2,0,1:T(8,128)(2,1)S(1)} %copy.41), channel_id=1, source_target_pairs={{0,8},{8,16},{16,24},{24,32},{32,40},{40,48},{48,56},{56,64},{64,7... | collective-permute-start | bytes 1572872 | tf_op jit(solution)/shard_map/while/body/eval_jaxpr/ppermute | solution.py:10
  186.4 12.9 %collective-permute-start.1 = (bf16[1024,2,128]{2,0,1:T(8,128)(2,1)S(1)}, bf16[1024,2,128]{2,0,1:T(8,128)(2,1)S(1)}, u32[]{:S(2)}, u32[]{:S(2)}) collective-permute-start(bf16[1024,2,128]{2,0,1:T(8,128)(2,1)S(1)} %copy.41), channel_id=1, source_target_pairs={{0,8},{8,16},{16,24},{24,32},{32,40},{40,48},{48,56},{56,64},{64,7... | collective-permute-start | bytes 1572872 | tf_op jit(solution)/shard_map/while/body/eval_jaxpr/ppermute | solution.py:10
  199.3 12.9 %collective-permute-start.1 = (bf16[1024,2,128]{2,0,1:T(8,128)(2,1)S(1)}, bf16[1024,2,128]{2,0,1:T(8,128)(2,1)S(1)}, u32[]{:S(2)}, u32[]{:S(2)}) collective-permute-start(bf16[1024,2,128]{2,0,1:T(8,128)(2,1)S(1)} %copy.41), channel_id=1, source_target_pairs={{0,8},{8,16},{16,24},{24,32},{32,40},{40,48},{48,56},{56,64},{64,7... | collective-permute-start | bytes 1572872 | tf_op jit(solution)/shard_map/while/body/eval_jaxpr/ppermute | solution.py:10
  212.3 12.9 %collective-permute-start.1 = (bf16[1024,2,128]{2,0,1:T(8,128)(2,1)S(1)}, bf16[1024,2,128]{2,0,1:T(8,128)(2,1)S(1)}, u32[]{:S(2)}, u32[]{:S(2)}) collective-permute-start(bf16[1024,2,128]{2,0,1:T(8,128)(2,1)S(1)} %copy.41), channel_id=1, source_target_pairs={{0,8},{8,16},{16,24},{24,32},{32,40},{40,48},{48,56},{56,64},{64,7... | collective-permute-start | bytes 1572872 | tf_op jit(solution)/shard_map/while/body/eval_jaxpr/ppermute | solution.py:10
  225.2 12.9 %collective-permute-start.1 = (bf16[1024,2,128]{2,0,1:T(8,128)(2,1)S(1)}, bf16[1024,2,128]{2,0,1:T(8,128)(2,1)S(1)}, u32[]{:S(2)}, u32[]{:S(2)}) collective-permute-start(bf16[1024,2,128]{2,0,1:T(8,128)(2,1)S(1)} %copy.41), channel_id=1, source_target_pairs={{0,8},{8,16},{16,24},{24,32},{32,40},{40,48},{48,56},{56,64},{64,7... | collective-permute-start | bytes 1572872 | tf_op jit(solution)/shard_map/while/body/eval_jaxpr/ppermute | solution.py:10
  243.5 152.0 %copy-start = (s32[4]{0:T(128)S(1)}, s32[4]{0:T(128)}, u32[]{:S(2)}) copy-start(s32[4]{0:T(128)} %constant.181.clone.1) | copy-start | bytes 52
  243.5 147.9 %all-gather.2.cloned.1.call-start = ((), (), s32[]{:S(2)}) async-start(), calls=%async_computation.3 | async-start | bytes 2359296 | tf_op jit(solution)/shard_map/all_gather | solution.py:104
  339.1 406.1 %reduce-scatter.5.cloned.1.call-start = ((), (), s32[]{:S(2)}) async-start(), calls=%async_computation.4 | async-start | bytes 69632 | tf_op jit(solution)/shard_map/reduce_scatter | solution.py:112
  395.5 362.1 %copy-start.2 = (s32[2,8]{1,0:T(2,128)S(1)}, s32[2,8]{1,0:T(2,128)}, u32[]{:S(2)}) copy-start(s32[2,8]{1,0:T(2,128)} %param.17) | copy-start | bytes 196
  395.6 364.4 %copy-start.1 = (bf16[2,8,128]{2,1,0:T(8,128)(2,1)S(1)}, bf16[2,8,128]{2,1,0:T(8,128)(2,1)}, u32[]{:S(2)}) copy-start(bf16[2,8,128]{2,1,0:T(8,128)(2,1)} %param.15) | copy-start | bytes 12292
  397.5 18.5 %collective-permute-start = (bf16[1024,2,128]{2,0,1:T(8,128)(2,1)}, bf16[1024,2,128]{2,0,1:T(8,128)(2,1)}, u32[]{:S(2)}, u32[]{:S(2)}) collective-permute-start(bf16[1024,2,128]{2,0,1:T(8,128)(2,1)} %copy.50), channel_id=1, source_target_pairs={{0,8},{8,16},{16,24},{24,32},{32,40},{40,48},{48,56},{56,64},{64,7... | collective-permute-start | bytes 1572872 | tf_op jit(solution)/shard_map/while/body/eval_jaxpr/ppermute | solution.py:10
  417.9 15.4 %collective-permute-start = (bf16[1024,2,128]{2,0,1:T(8,128)(2,1)}, bf16[1024,2,128]{2,0,1:T(8,128)(2,1)}, u32[]{:S(2)}, u32[]{:S(2)}) collective-permute-start(bf16[1024,2,128]{2,0,1:T(8,128)(2,1)} %copy.50), channel_id=1, source_target_pairs={{0,8},{8,16},{16,24},{24,32},{32,40},{40,48},{48,56},{56,64},{64,7... | collective-permute-start | bytes 1572872 | tf_op jit(solution)/shard_map/while/body/eval_jaxpr/ppermute | solution.py:10
  435.2 17.2 %collective-permute-start = (bf16[1024,2,128]{2,0,1:T(8,128)(2,1)}, bf16[1024,2,128]{2,0,1:T(8,128)(2,1)}, u32[]{:S(2)}, u32[]{:S(2)}) collective-permute-start(bf16[1024,2,128]{2,0,1:T(8,128)(2,1)} %copy.50), channel_id=1, source_target_pairs={{0,8},{8,16},{16,24},{24,32},{32,40},{40,48},{48,56},{56,64},{64,7... | collective-permute-start | bytes 1572872 | tf_op jit(solution)/shard_map/while/body/eval_jaxpr/ppermute | solution.py:10
  454.3 15.4 %collective-permute-start = (bf16[1024,2,128]{2,0,1:T(8,128)(2,1)}, bf16[1024,2,128]{2,0,1:T(8,128)(2,1)}, u32[]{:S(2)}, u32[]{:S(2)}) collective-permute-start(bf16[1024,2,128]{2,0,1:T(8,128)(2,1)} %copy.50), channel_id=1, source_target_pairs={{0,8},{8,16},{16,24},{24,32},{32,40},{40,48},{48,56},{56,64},{64,7... | collective-permute-start | bytes 1572872 | tf_op jit(solution)/shard_map/while/body/eval_jaxpr/ppermute | solution.py:10
  471.6 18.1 %collective-permute-start = (bf16[1024,2,128]{2,0,1:T(8,128)(2,1)}, bf16[1024,2,128]{2,0,1:T(8,128)(2,1)}, u32[]{:S(2)}, u32[]{:S(2)}) collective-permute-start(bf16[1024,2,128]{2,0,1:T(8,128)(2,1)} %copy.50), channel_id=1, source_target_pairs={{0,8},{8,16},{16,24},{24,32},{32,40},{40,48},{48,56},{56,64},{64,7... | collective-permute-start | bytes 1572872 | tf_op jit(solution)/shard_map/while/body/eval_jaxpr/ppermute | solution.py:10
  491.6 15.4 %collective-permute-start = (bf16[1024,2,128]{2,0,1:T(8,128)(2,1)}, bf16[1024,2,128]{2,0,1:T(8,128)(2,1)}, u32[]{:S(2)}, u32[]{:S(2)}) collective-permute-start(bf16[1024,2,128]{2,0,1:T(8,128)(2,1)} %copy.50), channel_id=1, source_target_pairs={{0,8},{8,16},{16,24},{24,32},{32,40},{40,48},{48,56},{56,64},{64,7... | collective-permute-start | bytes 1572872 | tf_op jit(solution)/shard_map/while/body/eval_jaxpr/ppermute | solution.py:10
  508.9 17.2 %collective-permute-start = (bf16[1024,2,128]{2,0,1:T(8,128)(2,1)}, bf16[1024,2,128]{2,0,1:T(8,128)(2,1)}, u32[]{:S(2)}, u32[]{:S(2)}) collective-permute-start(bf16[1024,2,128]{2,0,1:T(8,128)(2,1)} %copy.50), channel_id=1, source_target_pairs={{0,8},{8,16},{16,24},{24,32},{32,40},{40,48},{48,56},{56,64},{64,7... | collective-permute-start | bytes 1572872 | tf_op jit(solution)/shard_map/while/body/eval_jaxpr/ppermute | solution.py:10
  528.0 15.4 %collective-permute-start = (bf16[1024,2,128]{2,0,1:T(8,128)(2,1)}, bf16[1024,2,128]{2,0,1:T(8,128)(2,1)}, u32[]{:S(2)}, u32[]{:S(2)}) collective-permute-start(bf16[1024,2,128]{2,0,1:T(8,128)(2,1)} %copy.50), channel_id=1, source_target_pairs={{0,8},{8,16},{16,24},{24,32},{32,40},{40,48},{48,56},{56,64},{64,7... | collective-permute-start | bytes 1572872 | tf_op jit(solution)/shard_map/while/body/eval_jaxpr/ppermute | solution.py:10
  545.3 18.1 %collective-permute-start = (bf16[1024,2,128]{2,0,1:T(8,128)(2,1)}, bf16[1024,2,128]{2,0,1:T(8,128)(2,1)}, u32[]{:S(2)}, u32[]{:S(2)}) collective-permute-start(bf16[1024,2,128]{2,0,1:T(8,128)(2,1)} %copy.50), channel_id=1, source_target_pairs={{0,8},{8,16},{16,24},{24,32},{32,40},{40,48},{48,56},{56,64},{64,7... | collective-permute-start | bytes 1572872 | tf_op jit(solution)/shard_map/while/body/eval_jaxpr/ppermute | solution.py:10
  565.3 15.4 %collective-permute-start = (bf16[1024,2,128]{2,0,1:T(8,128)(2,1)}, bf16[1024,2,128]{2,0,1:T(8,128)(2,1)}, u32[]{:S(2)}, u32[]{:S(2)}) collective-permute-start(bf16[1024,2,128]{2,0,1:T(8,128)(2,1)} %copy.50), channel_id=1, source_target_pairs={{0,8},{8,16},{16,24},{24,32},{32,40},{40,48},{48,56},{56,64},{64,7... | collective-permute-start | bytes 1572872 | tf_op jit(solution)/shard_map/while/body/eval_jaxpr/ppermute | solution.py:10
  582.6 16.9 %collective-permute-start = (bf16[1024,2,128]{2,0,1:T(8,128)(2,1)}, bf16[1024,2,128]{2,0,1:T(8,128)(2,1)}, u32[]{:S(2)}, u32[]{:S(2)}) collective-permute-start(bf16[1024,2,128]{2,0,1:T(8,128)(2,1)} %copy.50), channel_id=1, source_target_pairs={{0,8},{8,16},{16,24},{24,32},{32,40},{40,48},{48,56},{56,64},{64,7... | collective-permute-start | bytes 1572872 | tf_op jit(solution)/shard_map/while/body/eval_jaxpr/ppermute | solution.py:10
  601.4 15.4 %collective-permute-start = (bf16[1024,2,128]{2,0,1:T(8,128)(2,1)}, bf16[1024,2,128]{2,0,1:T(8,128)(2,1)}, u32[]{:S(2)}, u32[]{:S(2)}) collective-permute-start(bf16[1024,2,128]{2,0,1:T(8,128)(2,1)} %copy.50), channel_id=1, source_target_pairs={{0,8},{8,16},{16,24},{24,32},{32,40},{40,48},{48,56},{56,64},{64,7... | collective-permute-start | bytes 1572872 | tf_op jit(solution)/shard_map/while/body/eval_jaxpr/ppermute | solution.py:10
  618.7 18.1 %collective-permute-start = (bf16[1024,2,128]{2,0,1:T(8,128)(2,1)}, bf16[1024,2,128]{2,0,1:T(8,128)(2,1)}, u32[]{:S(2)}, u32[]{:S(2)}) collective-permute-start(bf16[1024,2,128]{2,0,1:T(8,128)(2,1)} %copy.50), channel_id=1, source_target_pairs={{0,8},{8,16},{16,24},{24,32},{32,40},{40,48},{48,56},{56,64},{64,7... | collective-permute-start | bytes 1572872 | tf_op jit(solution)/shard_map/while/body/eval_jaxpr/ppermute | solution.py:10
  638.8 15.4 %collective-permute-start = (bf16[1024,2,128]{2,0,1:T(8,128)(2,1)}, bf16[1024,2,128]{2,0,1:T(8,128)(2,1)}, u32[]{:S(2)}, u32[]{:S(2)}) collective-permute-start(bf16[1024,2,128]{2,0,1:T(8,128)(2,1)} %copy.50), channel_id=1, source_target_pairs={{0,8},{8,16},{16,24},{24,32},{32,40},{40,48},{48,56},{56,64},{64,7... | collective-permute-start | bytes 1572872 | tf_op jit(solution)/shard_map/while/body/eval_jaxpr/ppermute | solution.py:10
  656.0 15.4 %collective-permute-start = (bf16[1024,2,128]{2,0,1:T(8,128)(2,1)}, bf16[1024,2,128]{2,0,1:T(8,128)(2,1)}, u32[]{:S(2)}, u32[]{:S(2)}) collective-permute-start(bf16[1024,2,128]{2,0,1:T(8,128)(2,1)} %copy.50), channel_id=1, source_target_pairs={{0,8},{8,16},{16,24},{24,32},{32,40},{40,48},{48,56},{56,64},{64,7... | collective-permute-start | bytes 1572872 | tf_op jit(solution)/shard_map/while/body/eval_jaxpr/ppermute | solution.py:10
  673.3 15.4 %collective-permute-start = (bf16[1024,2,128]{2,0,1:T(8,128)(2,1)}, bf16[1024,2,128]{2,0,1:T(8,128)(2,1)}, u32[]{:S(2)}, u32[]{:S(2)}) collective-permute-start(bf16[1024,2,128]{2,0,1:T(8,128)(2,1)} %copy.50), channel_id=1, source_target_pairs={{0,8},{8,16},{16,24},{24,32},{32,40},{40,48},{48,56},{56,64},{64,7... | collective-permute-start | bytes 1572872 | tf_op jit(solution)/shard_map/while/body/eval_jaxpr/ppermute | solution.py:10
  745.9 3.5 collective-permute-start.2
  749.3 4.0 collective-permute-start.3
  753.4 2.5 collective-permute-start.4
  755.9 4.0 collective-permute-start.5
Sparse Core Ops, SparseCore 0:
  243.6 93.3 reduce-scatter.2
  339.3 52.1 all-gather.1
  689.5 55.6 reduce-scatter.4
where the time goes:
time: 774 us; the launch traced here: 767 us
  local copies, waits for them, and re-layouts  241 us (31%)
  waiting for transfers between devices  207 us (27%)
  starting transfers between devices  122 us (16%)
  matrix products  114 us (15%)
  other arithmetic  38.9 us (5%)
  blocking collectives  26.2 us (3%)
  between operations  13.8 us (2%)
    ppermute x32, starting transfers between devices, shifted(): return lax.ppermute(array, axis, pairs)  115 us
    reduce_scatter x1, waiting for transfers between devices, body(): lax.psum_scatter(upgoing_part, 'src', scatter_dimension=0, tiled=True)  92.5 us
    dot_general x16, matrix products, forward_term(): jnp.einsum('kne,njea->kja', block_of_lags, reflection_matrix, preferred_e...  76.3 us
    reshape x16, local copies, waits for them, and re-layouts, shear_sum(): flat_rows.reshape(source_count, focal_count, lag_len, 2 * lag_len + 1)  59.3 us
    reduce_scatter x1, waiting for transfers between devices, body(): lax.psum_scatter(blocks.astype(jnp.bfloat16), 'lag', scatter_dimension=0,...  55.9 us
    reshape x16, local copies, waits for them, and re-layouts, toeplitz(): flat_rows.reshape(source_count, focal_count, lag_len, 2 * lag_len - 1)  53.7 us
    all_gather x1, waiting for transfers between devices, body(): full_minus_field = lax.all_gather(focus_minus, 'src', axis=0, tiled=True)  52.2 us
    dot_general x16, matrix products, backward_term(): jnp.einsum('exq,enc->xnqc', block_of_lags, full_minus_field, preferred_el...  38.2 us
  transfers between devices with their start and end apart: 39, of which 7 were waited for; matrix products, arithmetic and copies ran while one was open for 45% of the time, Pallas kernels for 0%

commit v1 on v0

v1 whole, which is shorter than its diff:
```python
import functools
import math

import jax
import jax.numpy as jnp
import numpy as np
from jax import lax
from jax.experimental import pallas as pl
from jax.experimental.pallas import tpu as pltpu
from jax.sharding import PartitionSpec as P

MESH = pl.DeviceIdType.MESH
LAGS, SRCS = 16, 8
J = 128
BLOCKS = 16
RADIX = 32
HALF = RADIX // 2 + 1
TOTAL = RADIX * J
F32, BF16 = jnp.float32, jnp.bfloat16


def add(a, b):
    if a is None or b is None:
        return b if a is None else a
    return a + b


def sub(a, b):
    if b is None:
        return a
    return -b if a is None else a - b


def neg(a):
    return None if a is None else -a


def scale(a, c):
    if a is None or c == 0.0:
        return None
    if c == 1.0:
        return a
    return -a if c == -1.0 else a * c


def root(n, k, sign):
    k = k % n
    if 4 * k % n == 0:
        c, s = [(1.0, 0.0), (0.0, 1.0), (-1.0, 0.0), (0.0, -1.0)][4 * k // n]
    else:
        c, s = math.cos(2 * math.pi * k / n), math.sin(2 * math.pi * k / n)
    return c, sign * s


def times(z, w):
    (re, im), (c, s) = z, w
    if re is not None and im is not None and abs(abs(c) - abs(s)) < 1e-12:
        h = abs(c)
        a, b = math.copysign(1.0, c), math.copysign(1.0, s)
        first = re if a > 0 else -re
        second = re if b > 0 else -re
        return (
            (first - im if b > 0 else first + im) * h,
            (second + im if a > 0 else second - im) * h,
        )
    return sub(scale(re, c), scale(im, s)), add(scale(re, s), scale(im, c))


def cadd(a, b):
    return add(a[0], b[0]), add(a[1], b[1])


def csub(a, b):
    return sub(a[0], b[0]), sub(a[1], b[1])


def cfft(values, sign):
    n = len(values)
    if n == 1:
        return values
    even, odd = cfft(values[0::2], sign), cfft(values[1::2], sign)
    odd = [times(v, root(n, k, sign)) for k, v in enumerate(odd)]
    return [cadd(a, b) for a, b in zip(even, odd)] + [csub(a, b) for a, b in zip(even, odd)]


def real_fft(x):
    n = len(x)
    if n == 1:
        return [(x[0], None)]
    half = n // 2
    z = [add(x[p], x[p + half]) for p in range(half)]
    d = [sub(x[p], x[p + half]) for p in range(half)]
    out = [None] * (half + 1)
    if n == 2:
        return [(z[0], None), (d[0], None)]
    out[0::2] = real_fft(z)
    quarter = n // 4
    turned = [times((d[p], neg(d[p + quarter])), root(n, p, -1)) for p in range(quarter)]
    for q, v in enumerate(cfft(turned, -1)):
        k = 4 * q + 1
        if k <= half:
            out[k] = v
        else:
            out[n - k] = (v[0], neg(v[1]))
    return out


def real_sum(spectrum):
    n = 2 * (len(spectrum) - 1)
    half = n // 2
    if n == 2:
        return [spectrum[0][0] + spectrum[1][0], spectrum[0][0] - spectrum[1][0]]
    even = real_sum(spectrum[0::2])
    quarter = n // 4
    terms = []
    for q in range(quarter):
        k = 4 * q + 1
        terms.append(spectrum[k] if k <= half else (spectrum[n - k][0], -spectrum[n - k][1]))
    turned = [times(v, root(n, p, 1)) for p, v in enumerate(cfft(terms, 1))]
    odd = [v[0] for v in turned] + [-v[1] for v in turned]
    if n == RADIX:
        return [even[p] + odd[p] for p in range(half)]
    return [even[p] + odd[p] for p in range(half)] + [even[p] - odd[p] for p in range(half)]


def split(matrix):
    high = matrix.astype(np.float32).astype(BF16)
    low = (matrix - high.astype(np.float64)).astype(np.float32).astype(BF16)
    return np.stack([high, low])


def as_real(matrix):
    return np.block([[matrix.real, matrix.imag], [-matrix.imag, matrix.real]])


@functools.cache
def tables():
    j = np.arange(J)
    k1 = np.arange(HALF)
    weight = np.where((k1 == 0) | (k1 == RADIX // 2), 1.0, 2.0)[:, None]
    forward = np.exp(-2j * np.pi * np.outer(j, j) / J)
    inverse = np.exp(2j * np.pi * np.outer(j, j) / J) / TOTAL
    turn = np.exp(-2j * np.pi * np.outer(k1, j) / TOTAL)
    back = weight * turn.conj()
    matrices = np.stack(
        [split(as_real(m)) for m in (forward, inverse, inverse[:, ::-1])]
    )
    turns = np.stack([np.stack([t.real, t.imag], 1) for t in (turn, back, back[:, ::-1])])
    return matrices, turns.reshape(3 * HALF * 2, J).astype(np.float32)


def turn_rows(turn_ref, which, k):
    at = (which * HALF + k) * 2
    return (
        jnp.broadcast_to(turn_ref[at : at + 1, :], (8, J)),
        jnp.broadcast_to(turn_ref[at + 1 : at + 2, :], (8, J)),
    )


def store_spectrum(turn_ref, blocks, ref, rows):
    for k, (re, im) in enumerate(real_fft(list(blocks) + [None] * (RADIX - BLOCKS))):
        if k == 0:
            im = jnp.zeros_like(re)
        else:
            c, s = turn_rows(turn_ref, 0, k)
            if im is None:
                re, im = re * c, re * s
            else:
                re, im = re * c - im * s, re * s + im * c
        ref[k, rows, 0:J] = re
        ref[k, rows, J : 2 * J] = im


def load_blocks(turn_ref, which, ref, rows):
    spectrum = []
    for k in range(HALF):
        re, im = ref[k, rows, 0:J], ref[k, rows, J : 2 * J]
        if k == 0:
            spectrum.append((re, None))
            continue
        c, s = turn_rows(turn_ref, which, k)
        if k == RADIX // 2:
            spectrum.append((re * c - im * s, None))
        else:
            spectrum.append((re * c - im * s, re * s + im * c))
    return real_sum(spectrum)


def product(a, mat_ref, which):
    high = a.astype(BF16)
    low = (a - high.astype(F32)).astype(BF16)
    dot = functools.partial(jnp.dot, preferred_element_type=F32)
    return dot(high, mat_ref[which, 0]) + dot(low, mat_ref[which, 0]) + dot(high, mat_ref[which, 1])


def row_of(r, s):
    return (s // 2) * 16 + r * 2 + s % 2


def local_kernel(refl_ref, plus_ref, onset_ref, mat_ref, turn_ref, minus_ref, corr_ref, a_ref, h_ref, u_ref, c_ref):
    def spectra(g, carry):
        for source, base in ((refl_ref, 0), (plus_ref, 128)):
            values = [source[g, p].astype(F32) for p in range(BLOCKS)]
            for half in range(2):
                rows = pl.ds(pl.multiple_of(base + 16 * g + 8 * half, 8), 8)
                store_spectrum(turn_ref, [v[8 * half : 8 * half + 8] for v in values], a_ref, rows)
        return carry

    lax.fori_loop(0, SRCS, spectra, 0)

    def forward(k, carry):
        h_ref[k] = product(a_ref[k], mat_ref, 0)
        for first in range(0, 8, 4):
            acc = [None] * 4
            for s in range(16):
                at = 128 + 8 * s
                fr, fi = h_ref[k, at : at + 8, 0:J], h_ref[k, at : at + 8, J : 2 * J]
                for i in range(4):
                    row = row_of(first + i, s)
                    rr = jnp.broadcast_to(h_ref[k, row : row + 1, 0:J], (8, J))
                    ri = jnp.broadcast_to(h_ref[k, row : row + 1, J : 2 * J], (8, J))
                    term = (rr * fr - ri * fi, rr * fi + ri * fr)
                    acc[i] = term if acc[i] is None else cadd(acc[i], term)
            for i in range(4):
                at = 8 * (first + i)
                u_ref[k, at : at + 8, 0:J] = acc[i][0]
                u_ref[k, at : at + 8, J : 2 * J] = acc[i][1]
        u_ref[k] = product(u_ref[k], mat_ref, 1)
        return carry

    lax.fori_loop(0, HALF, forward, 0)

    sample = lax.broadcasted_iota(jnp.int32, (8, J), 1)

    def middle(pair, carry):
        kept = []
        for half in range(2):
            rows = pl.ds(pl.multiple_of(16 * pair + 8 * half, 8), 8)
            onset = onset_ref[rows, :]
            low, high = BLOCKS * J // 2 - onset, BLOCKS * J // 2 - 1 + onset
            blocks = []
            for p, x in enumerate(load_blocks(turn_ref, 1, u_ref, rows)):
                n = sample + p * J
                x = jnp.where((n >= low) & (n <= high), x, 0.0)
                blocks.append(x.astype(BF16).astype(F32))
            kept.append(blocks)
            store_spectrum(turn_ref, blocks, a_ref, rows)
        for p in range(BLOCKS):
            both = jnp.concatenate([kept[0][p], kept[1][p]], axis=0).astype(BF16)
            minus_ref[p, pl.ds(pl.multiple_of(16 * pair, 16), 16), :] = both
        return carry

    lax.fori_loop(0, 4, middle, 0)

    def backward(k, carry):
        u_ref[k] = product(a_ref[k, 0:64], mat_ref, 0)
        for first in range(0, 16, 4):
            acc = [None] * 4
            for r in range(8):
                mr, mi = u_ref[k, 8 * r : 8 * r + 8, 0:J], u_ref[k, 8 * r : 8 * r + 8, J : 2 * J]
                for i in range(4):
                    row = row_of(r, first + i)
                    rr = jnp.broadcast_to(h_ref[k, row : row + 1, 0:J], (8, J))
                    ri = jnp.broadcast_to(h_ref[k, row : row + 1, J : 2 * J], (8, J))
                    term = (rr * mr + ri * mi, rr * mi - ri * mr)
                    acc[i] = term if acc[i] is None else cadd(acc[i], term)
            for i in range(4):
                at = 8 * (first + i)
                c_ref[k, at : at + 8, 0:J] = acc[i][0]
                c_ref[k, at : at + 8, J : 2 * J] = acc[i][1]
        c_ref[k] = product(c_ref[k], mat_ref, 2)
        return carry

    lax.fori_loop(0, HALF, backward, 0)

    def last(g, carry):
        kept = []
        for half in range(2):
            rows = pl.ds(pl.multiple_of(16 * g + 8 * half, 8), 8)
            kept.append(load_blocks(turn_ref, 2, c_ref, rows))
        for p in range(BLOCKS):
            both = jnp.concatenate([kept[0][BLOCKS - 1 - p], kept[1][BLOCKS - 1 - p]], axis=0)
            corr_ref[g, p] = both.astype(BF16)
        return carry

    lax.fori_loop(0, SRCS, last, 0)


def position():
    return lax.axis_index("lag"), lax.axis_index("src")


def partner(i, my_lag, my_src):
    return (my_lag + i // SRCS) % LAGS, (my_src + i % SRCS) % SRCS


def greet(barrier, my_lag, my_src):
    def signal(i, carry):
        pl.semaphore_signal(barrier, inc=1, device_id=partner(i, my_lag, my_src), device_id_type=MESH)
        return carry

    lax.fori_loop(1, LAGS * SRCS, signal, 0)
    pl.semaphore_wait(barrier, LAGS * SRCS - 1)


def spread_kernel(refl_ref, plus_ref, refl_out, plus_out, sems):
    my_lag, my_src = position()
    chip, core = my_lag // 2, my_lag % 2
    greet(pltpu.get_barrier_semaphore(), my_lag, my_src)

    def remote(source, target, send, recv, where):
        pltpu.make_async_remote_copy(
            src_ref=source, dst_ref=target, send_sem=sems.at[send], recv_sem=sems.at[recv],
            device_id=where, device_id_type=MESH,
        ).start()

    for i in range(1, SRCS):
        remote(plus_ref, plus_out.at[my_src, chip, core], 2, 3, (my_lag, (my_src + i) % SRCS))
    pltpu.make_async_copy(plus_ref, plus_out.at[my_src, chip, core], sems.at[3]).start()

    def send(i, carry):
        lag, src = partner(i, my_lag, my_src)
        remote(refl_ref.at[src, lag], refl_out.at[my_src, my_lag], 0, 1, (lag, src))
        return carry

    lax.fori_loop(1, LAGS * SRCS, send, 0)
    pltpu.make_async_copy(refl_ref.at[my_src, my_lag], refl_out.at[my_src, my_lag], sems.at[1]).start()

    def wait(ref, sem):
        pltpu.make_async_copy(ref, ref, sems.at[sem]).wait()

    wait(plus_out.at[:, chip, core], 3)
    mine = plus_out.at[:, chip, core]
    for i in range(1, LAGS // 2):
        remote(mine, mine, 4, 5, ((my_lag + 2 * i) % LAGS, my_src))
    wait(plus_out.at[:, pl.ds(0, 7), 0], 5)
    half = plus_out.at[:, :, core]
    remote(half, half, 6, 7, (chip * 2 + 1 - core, my_src))
    wait(half, 7)
    wait(refl_out, 1)
    wait(plus_out.at[pl.ds(0, 7), 0, 0], 2)
    wait(plus_out.at[:, pl.ds(0, 7), 0], 4)
    wait(half, 6)
    wait(refl_out.at[pl.ds(0, 127 // 16 * 1)], 0)
    wait(refl_out.at[0, pl.ds(0, 15)], 0)


def gather_kernel(minus_ref, corr_ref, start_ref, onset_ref, minus_out, next_out, parts, sems):
    my_lag, my_src = position()
    greet(pltpu.get_barrier_semaphore(), my_lag, my_src)

    def remote(source, target, send, recv, where):
        pltpu.make_async_remote_copy(
            src_ref=source, dst_ref=target, send_sem=sems.at[send], recv_sem=sems.at[recv],
            device_id=where, device_id_type=MESH,
        ).start()

    for i in range(1, LAGS):
        lag = (my_lag + i) % LAGS
        remote(minus_ref.at[lag], minus_out.at[my_lag], 2, 3, (lag, my_src))
    pltpu.make_async_copy(minus_ref.at[my_lag], minus_out.at[my_lag], sems.at[3]).start()

    def send(i, carry):
        lag, src = partner(i, my_lag, my_src)
        remote(corr_ref.at[src, lag], parts.at[my_src, my_lag], 0, 1, (lag, src))
        return carry

    lax.fori_loop(1, LAGS * SRCS, send, 0)
    pltpu.make_async_copy(corr_ref.at[my_src, my_lag], parts.at[my_src, my_lag], sems.at[1]).start()

    def wait(ref, sem):
        pltpu.make_async_copy(ref, ref, sems.at[sem]).wait()

    wait(parts, 1)
    total = jnp.zeros((16, J), F32)
    for g in range(SRCS):
        for l in range(LAGS):
            total = total + parts[g, l].astype(F32)
    n = lax.broadcasted_iota(jnp.int32, (16, J), 1) + my_lag * J
    onset = onset_ref[...]
    inside = (n >= BLOCKS * J // 2 - onset) & (n <= BLOCKS * J // 2 - 1 + onset)
    next_out[...] = start_ref[...].astype(F32) + jnp.where(inside, total, 0.0)
    wait(minus_out, 3)
    wait(minus_out.at[pl.ds(0, 15)], 2)
    wait(parts.at[pl.ds(0, 7)], 0)
    wait(parts.at[0, pl.ds(0, 15)], 0)


def body(reflection, focus_plus, focus_start, onset_receiver, onset_source):
    vmem = pl.BlockSpec(memory_space=pltpu.VMEM)
    share = lax.axis_index("src") * 128 + lax.axis_index("lag") * 8
    onset = lax.dynamic_slice_in_dim(onset_receiver, share, 8, 0)
    onset = jnp.broadcast_to(onset.reshape(64, 1), (64, J))
    onset_s = jnp.broadcast_to(onset_source.reshape(16, 1), (16, J))
    matrices, turns = tables()

    refl, plus = pl.pallas_call(
        spread_kernel,
        out_shape=(
            jax.ShapeDtypeStruct((SRCS, LAGS, 16, J), BF16),
            jax.ShapeDtypeStruct((SRCS, LAGS // 2, 2, 16, J), BF16),
        ),
        in_specs=[vmem, vmem],
        out_specs=(vmem, vmem),
        scratch_shapes=[pltpu.SemaphoreType.DMA((8,))],
        compiler_params=pltpu.CompilerParams(
            collective_id=0, has_side_effects=True, vmem_limit_bytes=32 * 2**20
        ),
        name="spread",
    )(reflection.reshape(SRCS, LAGS, 16, J), focus_plus.reshape(16, J))

    minus, corr = pl.pallas_call(
        local_kernel,
        out_shape=(
            jax.ShapeDtypeStruct((BLOCKS, 64, J), BF16),
            jax.ShapeDtypeStruct((SRCS, LAGS, 16, J), BF16),
        ),
        in_specs=[vmem] * 5,
        out_specs=(vmem, vmem),
        scratch_shapes=[
            pltpu.VMEM((HALF, 256, 2 * J), F32),
            pltpu.VMEM((HALF, 256, 2 * J), F32),
            pltpu.VMEM((HALF, 64, 2 * J), F32),
            pltpu.VMEM((HALF, 128, 2 * J), F32),
        ],
        compiler_params=pltpu.CompilerParams(vmem_limit_bytes=48 * 2**20),
        name="local",
    )(refl, plus.reshape(SRCS, LAGS, 16, J), onset, jnp.asarray(matrices), jnp.asarray(turns))

    minus_out, next_out = pl.pallas_call(
        gather_kernel,
        out_shape=(
            jax.ShapeDtypeStruct((LAGS, 64, J), BF16),
            jax.ShapeDtypeStruct((16, J), F32),
        ),
        in_specs=[vmem] * 4,
        out_specs=(vmem, vmem),
        scratch_shapes=[pltpu.VMEM((SRCS, LAGS, 16, J), BF16), pltpu.SemaphoreType.DMA((4,))],
        compiler_params=pltpu.CompilerParams(
            collective_id=1, has_side_effects=True, vmem_limit_bytes=32 * 2**20
        ),
        name="collect",
    )(minus, corr, focus_start.reshape(16, J), onset_s)
    return minus_out.reshape(128, 8, J), next_out.reshape(2, 8, J)


def solution(mesh):
    return jax.shard_map(
        body,
        mesh=mesh,
        in_specs=(
            P(None, "src", "lag"),
            P("src", None, "lag"),
            P("src", None, "lag"),
            P(),
            P("src", None),
        ),
        out_specs=(P("src", None, "lag"), P("src", None, "lag")),
        check_vma=False,
    )
```

time: 774 us -> 75 us (0.10)
  local copies, waits for them, and re-layouts: 241 us -> 6.58 us
  waiting for transfers between devices: 207 us -> 0 us
  starting transfers between devices: 122 us -> 0 us
  matrix products: 114 us -> 0 us
  Pallas kernels: 0 us -> 67.4 us
  other arithmetic: 38.9 us -> 0 us
  blocking collectives: 26.2 us -> 0 us
  between operations: 13.8 us -> 0.7 us
    reduce_scatter x2 -> x0, waiting for transfers between devices: 148 us -> none  [the longest x1 92.5 us: body(): lax.psum_scatter(upgoing_part, 'src', scatter_dimension=0, tiled=True)]
    reshape x48 -> x0, local copies, waits for them, and re-layouts: 141 us -> none  [the longest x16 59.3 us: shear_sum(): flat_rows.reshape(source_count, focal_count, lag_len, 2 * lag_len + 1)]
    ppermute x36 -> x0, starting transfers between devices: 122 us -> none  [the longest x32 115 us: shifted(): return lax.ppermute(array, axis, pairs)]
    dot_general x32 -> x0, matrix products: 114 us -> none  [the longest x16 76.3 us: forward_term(): jnp.einsum('kne,njea->kja', block_of_lags, reflection_matrix, preferred_e...]
    pallas_call x0 -> x3, Pallas kernels: none -> 67.4 us  [the longest x1 24.9 us: body(): pl.pallas_call(spread_kernel, out_shape=(jax.ShapeDtypeStruct((SRCS, LAGS...]
    all_gather x1 -> x0, waiting for transfers between devices: 52.2 us -> none  [body(): full_minus_field = lax.all_gather(focus_minus, 'src', axis=0, tiled=True)]
    another operation x16 -> x0, local copies, waits for them, and re-layouts: 30.1 us -> none
    all_gather x1 -> x0, blocking collectives: 26.2 us -> none  [body(): focus_all = lax.all_gather(focus_plus, 'lag', axis=2, tiled=True)]
  transfers between devices with their start and end apart: 39 -> 0, of which waited for: 7 -> 0; matrix products, arithmetic and copies ran while one was open for 45% -> 0% of each run, Pallas kernels for 0% -> 0%
where the time goes in v1:
time: 75 us; the launch traced here: 74.7 us
  Pallas kernels  67.4 us (90%)
  local copies, waits for them, and re-layouts  6.58 us (9%)
    pallas_call x1, Pallas kernels, body(): pl.pallas_call(spread_kernel, out_shape=(jax.ShapeDtypeStruct((SRCS, LAGS...  24.9 us
    pallas_call x1, Pallas kernels, body(): pl.pallas_call(local_kernel, out_shape=(jax.ShapeDtypeStruct((BLOCKS, 64,...  23.6 us
    pallas_call x1, Pallas kernels, body(): pl.pallas_call(gather_kernel, out_shape=(jax.ShapeDtypeStruct((LAGS, 64,...  18.9 us
    unnamed x16, local copies, waits for them, and re-layouts  6.13 us

profile of v1, /device:TPU:1, one launch (start us, length us, event | category | flops | bytes accessed | tf_op | source)
XLA Modules:
  0.0 74.7 jit_solution(5728908946939224103)
XLA Ops:
  0.6 0.0 copy-start
  0.7 0.7 copy-done
  1.4 0.1 constant_dynamic-slice_fusion
  1.5 0.1 copy.9
  1.5 0.1 broadcast_in_dim.14
  1.6 0.0 copy-start.4
  1.6 0.1 broadcast_in_dim.15.onset_ref
  1.7 0.6 copy-done.4
  2.3 0.0 copy-start.2
  2.3 1.0 %copy-done.2 = bf16[1024,2,128]{2,1,0:T(2,128)(2,1)S(1)} copy-done((bf16[1024,2,128]{2,1,0:T(2,128)(2,1)S(1)}, bf16[1024,2,128]{2,1,0:T(2,128)(2,1)}, u32[]{:S(2)}) %copy-start.2) | copy-done | bytes 524312
  3.4 0.0 copy-start.3
  3.4 24.9 %spread.1 = (bf16[8,16,16,128]{3,2,1,0:T(8,128)(2,1)S(1)}, bf16[8,8,2,16,128]{4,3,2,1,0:T(8,128)(2,1)S(1)}) custom-call(bf16[8,16,16,128]{3,2,1,0:T(8,128)(2,1)S(1)} %bitcast.6, bf16[16,128]{1,0:T(8,128)(2,1)S(1)} %bitcast.10), custom_call_target="tpu_custom_call" | custom-call | tf_op jit(solution)/shard_map/spread/pallas_call | solution.py:397
  28.2 0.0 copy-done.3
  28.2 0.0 copy-start.1
  28.3 1.1 %copy-done.1 = bf16[3,2,256,256]{3,2,1,0:T(8,128)(2,1)S(1)} copy-done((bf16[3,2,256,256]{3,2,1,0:T(8,128)(2,1)S(1)}, bf16[3,2,256,256]{3,2,1,0:T(8,128)(2,1)}, u32[]{:S(2)}) %copy-start.1) | copy-done | bytes 786456
  29.4 23.6 %local.1 = (bf16[16,64,128]{2,1,0:T(8,128)(2,1)S(1)}, bf16[8,16,16,128]{3,2,1,0:T(8,128)(2,1)S(1)}) custom-call(bf16[8,16,16,128]{3,2,1,0:T(8,128)(2,1)S(1)} %get-tuple-element.8.refl_ref, bf16[8,16,16,128]{3,2,1,0:T(8,128)(2,1)S(1)} %bitcast.7, s32[64,128]{1,0:T(8,128)S(1)} %broadcast_in_dim.15.onset_ref, bf16[3,2,256,256]{3,2,1,0:T(8,128)(2,1)S(1)} %copy-done.1, ...), custom_call_target="tpu_custom_call" | custom-call | tf_op jit(solution)/shard_map/local/pallas_call | solution.py:412
  53.0 0.0 copy-start.6
  53.0 0.7 copy-done.6
  53.7 0.1 broadcast_in_dim.16
  53.8 0.0 copy-start.5
  53.8 0.1 broadcast_in_dim.17.onset_ref
  53.8 0.6 copy-done.5
  54.4 18.9 %collect.1 = (bf16[16,64,128]{2,1,0:T(8,128)(2,1)S(1)}, f32[16,128]{1,0:T(8,128)S(1)}) custom-call(bf16[16,64,128]{2,1,0:T(8,128)(2,1)S(1)} %get-tuple-element.10.minus_ref, bf16[8,16,16,128]{3,2,1,0:T(8,128)(2,1)S(1)} %get-tuple-element.11.corr_ref, bf16[16,128]{1,0:T(8,128)(2,1)S(1)} %bitcast.11, s32[16,128]{1,0:T(8,128)S(1)} %broadcast_in_dim.17.onset_ref), custom_call_target="tpu_custom_call" | custom-call | tf_op jit(solution)/shard_map/collect/pallas_call | solution.py:430
  73.4 0.7 copy.12
  74.1 0.6 copy.13
Async XLA Ops:
  0.6 0.8 %copy-start = (s32[1024,8]{0,1:T(8,128)S(1)}, s32[1024,8]{0,1:T(8,128)}, u32[]{:S(2)}) copy-start(s32[1024,8]{0,1:T(8,128)} %param.10) | copy-start | bytes 98308
  1.6 0.7 copy-start.4
  2.3 1.0 %copy-start.2 = (bf16[1024,2,128]{2,1,0:T(2,128)(2,1)S(1)}, bf16[1024,2,128]{2,1,0:T(2,128)(2,1)}, u32[]{:S(2)}) copy-start(bf16[1024,2,128]{2,1,0:T(2,128)(2,1)} %param.7) | copy-start | bytes 1572868
  3.4 24.9 %copy-start.3 = (f32[102,128]{1,0:T(8,128)S(1)}, f32[102,128]{1,0:T(8,128)}, u32[]{:S(2)}) copy-start(f32[102,128]{1,0:T(8,128)} %constant.22.clone.turn_ref) | copy-start | bytes 156676
  28.2 1.1 %copy-start.1 = (bf16[3,2,256,256]{3,2,1,0:T(8,128)(2,1)S(1)}, bf16[3,2,256,256]{3,2,1,0:T(8,128)(2,1)}, u32[]{:S(2)}) copy-start(bf16[3,2,256,256]{3,2,1,0:T(8,128)(2,1)} %constant.21.clone.mat_ref) | copy-start | bytes 2359300
  53.0 0.7 copy-start.6
  53.8 0.7 copy-start.5

commit v2 on v1

v2 whole, which is shorter than its diff:
```python
import functools
import math

import jax
import jax.numpy as jnp
import numpy as np
from jax import lax
from jax.experimental import pallas as pl
from jax.experimental.pallas import tpu as pltpu
from jax.sharding import PartitionSpec as P

MESH = pl.DeviceIdType.MESH
LAGS, SRCS = 16, 8
CHIPS = LAGS // 2
RCV = 8
J = 128
BLOCKS = 16
RADIX = 32
HALF = RADIX // 2 + 1
TOTAL = RADIX * J
F32, BF16 = jnp.float32, jnp.bfloat16


def add(a, b):
    if a is None or b is None:
        return b if a is None else a
    return a + b


def sub(a, b):
    if b is None:
        return a
    return -b if a is None else a - b


def neg(a):
    return None if a is None else -a


def scale(a, c):
    if a is None or c == 0.0:
        return None
    if c == 1.0:
        return a
    return -a if c == -1.0 else a * c


def root(n, k, sign):
    k = k % n
    if 4 * k % n == 0:
        c, s = [(1.0, 0.0), (0.0, 1.0), (-1.0, 0.0), (0.0, -1.0)][4 * k // n]
    else:
        c, s = math.cos(2 * math.pi * k / n), math.sin(2 * math.pi * k / n)
    return c, sign * s


def times(z, w):
    (re, im), (c, s) = z, w
    if re is not None and im is not None and abs(abs(c) - abs(s)) < 1e-12:
        h = abs(c)
        a, b = math.copysign(1.0, c), math.copysign(1.0, s)
        first = re if a > 0 else -re
        second = re if b > 0 else -re
        return (
            (first - im if b > 0 else first + im) * h,
            (second + im if a > 0 else second - im) * h,
        )
    return sub(scale(re, c), scale(im, s)), add(scale(re, s), scale(im, c))


def cadd(a, b):
    return add(a[0], b[0]), add(a[1], b[1])


def csub(a, b):
    return sub(a[0], b[0]), sub(a[1], b[1])


def cfft(values, sign):
    n = len(values)
    if n == 1:
        return values
    even, odd = cfft(values[0::2], sign), cfft(values[1::2], sign)
    odd = [times(v, root(n, k, sign)) for k, v in enumerate(odd)]
    return [cadd(a, b) for a, b in zip(even, odd)] + [csub(a, b) for a, b in zip(even, odd)]


def real_fft(x):
    n = len(x)
    if n == 1:
        return [(x[0], None)]
    half = n // 2
    z = [add(x[p], x[p + half]) for p in range(half)]
    d = [sub(x[p], x[p + half]) for p in range(half)]
    out = [None] * (half + 1)
    if n == 2:
        return [(z[0], None), (d[0], None)]
    out[0::2] = real_fft(z)
    quarter = n // 4
    turned = [times((d[p], neg(d[p + quarter])), root(n, p, -1)) for p in range(quarter)]
    for q, v in enumerate(cfft(turned, -1)):
        k = 4 * q + 1
        if k <= half:
            out[k] = v
        else:
            out[n - k] = (v[0], neg(v[1]))
    return out


def real_sum(spectrum):
    n = 2 * (len(spectrum) - 1)
    half = n // 2
    if n == 2:
        return [spectrum[0][0] + spectrum[1][0], spectrum[0][0] - spectrum[1][0]]
    even = real_sum(spectrum[0::2])
    quarter = n // 4
    terms = []
    for q in range(quarter):
        k = 4 * q + 1
        terms.append(spectrum[k] if k <= half else (spectrum[n - k][0], -spectrum[n - k][1]))
    turned = [times(v, root(n, p, 1)) for p, v in enumerate(cfft(terms, 1))]
    odd = [v[0] for v in turned] + [-v[1] for v in turned]
    if n == RADIX:
        return [even[p] + odd[p] for p in range(half)]
    return [even[p] + odd[p] for p in range(half)] + [even[p] - odd[p] for p in range(half)]


def split(matrix):
    high = matrix.astype(np.float32).astype(BF16)
    low = (matrix - high.astype(np.float64)).astype(np.float32).astype(BF16)
    return np.stack([high, low])


def as_real(matrix):
    return np.block([[matrix.real, matrix.imag], [-matrix.imag, matrix.real]])


@functools.cache
def tables():
    j = np.arange(J)
    k1 = np.arange(HALF)
    weight = np.where((k1 == 0) | (k1 == RADIX // 2), 1.0, 2.0)[:, None]
    forward = np.exp(-2j * np.pi * np.outer(j, j) / J)
    inverse = np.exp(2j * np.pi * np.outer(j, j) / J) / TOTAL
    turn = np.exp(-2j * np.pi * np.outer(k1, j) / TOTAL)
    back = weight * turn.conj()
    matrices = np.stack(
        [split(as_real(m)) for m in (forward, inverse, inverse[:, ::-1])]
    )
    turns = np.stack([np.stack([t.real, t.imag], 1) for t in (turn, back, back[:, ::-1])])
    return matrices, turns.reshape(3 * HALF * 2, J).astype(np.float32)


def turn_rows(turn_ref, which, k):
    at = (which * HALF + k) * 2
    return (
        jnp.broadcast_to(turn_ref[at : at + 1, :], (8, J)),
        jnp.broadcast_to(turn_ref[at + 1 : at + 2, :], (8, J)),
    )


def store_spectrum(turn_ref, blocks, ref, rows):
    for k, (re, im) in enumerate(real_fft(list(blocks) + [None] * (RADIX - BLOCKS))):
        if k == 0:
            im = jnp.zeros_like(re)
        else:
            c, s = turn_rows(turn_ref, 0, k)
            if im is None:
                re, im = re * c, re * s
            else:
                re, im = re * c - im * s, re * s + im * c
        ref[k, rows, 0:J] = re
        ref[k, rows, J : 2 * J] = im


def load_blocks(turn_ref, which, ref, rows):
    spectrum = []
    for k in range(HALF):
        re, im = ref[k, rows, 0:J], ref[k, rows, J : 2 * J]
        if k == 0:
            spectrum.append((re, None))
            continue
        c, s = turn_rows(turn_ref, which, k)
        if k == RADIX // 2:
            spectrum.append((re * c - im * s, None))
        else:
            spectrum.append((re * c - im * s, re * s + im * c))
    return real_sum(spectrum)


def product(a, mat_ref, which):
    shape = a.shape
    a = a.reshape(shape[0] * shape[1], 2 * J)
    high = a.astype(BF16)
    low = (a - high.astype(F32)).astype(BF16)
    dot = functools.partial(jnp.dot, preferred_element_type=F32)
    out = dot(high, mat_ref[which, 0]) + dot(low, mat_ref[which, 0]) + dot(high, mat_ref[which, 1])
    return out.reshape(shape)


def transform(tile, a_ref, out_ref, mat_ref, turn_ref):
    values = [tile(p).astype(F32) for p in range(BLOCKS)]
    for half in range(2):
        rows = slice(8 * half, 8 * half + 8)
        store_spectrum(turn_ref, [v[rows] for v in values], a_ref, rows)
    out_ref[...] = product(a_ref[...], mat_ref, 0)


def both(ref, k, row):
    return (
        jnp.broadcast_to(ref[k, row : row + 1, 0:J], (8, J)),
        jnp.broadcast_to(ref[k, row : row + 1, J : 2 * J], (8, J)),
    )


def forward_terms(refl, plus, u_ref):
    def step(k, carry):
        f = [(plus[k, 8 * s : 8 * s + 8, 0:J], plus[k, 8 * s : 8 * s + 8, J : 2 * J]) for s in range(2)]
        for r in range(RCV):
            rows = slice(8 * r, 8 * r + 8)
            re, im = u_ref[k, rows, 0:J], u_ref[k, rows, J : 2 * J]
            for s in range(2):
                rr, ri = both(refl, k, 2 * r + s)
                fr, fi = f[s]
                re, im = re + (rr * fr - ri * fi), im + (rr * fi + ri * fr)
            u_ref[k, rows, 0:J] = re
            u_ref[k, rows, J : 2 * J] = im
        return carry

    lax.fori_loop(0, HALF, step, 0, unroll=True)


def backward_terms(refl, m_ref, c_ref):
    def step(k, carry):
        acc = [None, None]
        for r in range(RCV):
            rows = slice(8 * r, 8 * r + 8)
            mr, mi = m_ref[k, rows, 0:J], m_ref[k, rows, J : 2 * J]
            for s in range(2):
                rr, ri = both(refl, k, 2 * r + s)
                term = (rr * mr + ri * mi, rr * mi - ri * mr)
                acc[s] = term if acc[s] is None else cadd(acc[s], term)
        for s in range(2):
            c_ref[k, 8 * s : 8 * s + 8, 0:J] = acc[s][0]
            c_ref[k, 8 * s : 8 * s + 8, J : 2 * J] = acc[s][1]
        return carry

    lax.fori_loop(0, HALF, step, 0, unroll=True)


def window(onset, sample):
    return (sample >= BLOCKS * J // 2 - onset) & (sample <= BLOCKS * J // 2 - 1 + onset)


def middle(u_ref, a_ref, onset_ref, first, turn_ref, minus_ref):
    lane = lax.broadcasted_iota(jnp.int32, (8, J), 1)

    def step(pair, carry):
        kept = []
        for half in range(2):
            at = 2 * pair + half
            rows = pl.ds(pl.multiple_of(8 * at, 8), 8)
            mine = jnp.where(lane == first + at, onset_ref[...], 0).astype(F32)
            onset = jnp.broadcast_to(jnp.sum(mine, axis=1, keepdims=True), (8, J)).astype(jnp.int32)
            blocks = []
            for p, x in enumerate(load_blocks(turn_ref, 1, u_ref, rows)):
                blocks.append(jnp.where(window(onset, lane + p * J), x, 0.0).astype(BF16).astype(F32))
            kept.append(blocks)
            store_spectrum(turn_ref, blocks, a_ref, rows)
        for p in range(BLOCKS):
            joined = jnp.concatenate([kept[0][p], kept[1][p]], axis=0).astype(BF16)
            minus_ref[p, pl.ds(pl.multiple_of(16 * pair, 16), 16), :] = joined
        return carry

    lax.fori_loop(0, RCV // 2, step, 0)


def kernel(
    refl_ref, plus_ref, start_ref, onset_r_ref, onset_s_ref, mat_hbm, turn_hbm,
    minus_out, next_out,
    refl, plus, mats, turns, onset_r, onset_s, start,
    a_ref, hr_ref, hf_ref, u_ref, b_ref, m_ref, c_ref,
    minus, corr, peer, chip_sum, parts,
    local_sem, one_sem, refl_sem, peer_sem,
):
    my_lag, my_src = lax.axis_index("lag"), lax.axis_index("src")
    chip, core = lax.div(my_lag, 2), lax.rem(my_lag, 2)

    def remote(source, target, send, recv, where):
        pltpu.make_async_remote_copy(
            src_ref=source, dst_ref=target, send_sem=send, recv_sem=recv, device_id=where, device_id_type=MESH
        ).start()

    def wait(ref, sem):
        pltpu.make_async_copy(ref, ref, sem).wait()

    loads = [
        (mat_hbm, mats), (turn_hbm, turns), (start_ref, start), (onset_s_ref, onset_s),
        (onset_r_ref.at[:, pl.ds(pl.multiple_of(my_src * J, J), J)], onset_r),
    ]
    loads = [pltpu.make_async_copy(a, b, local_sem.at[i]) for i, (a, b) in enumerate(loads)]
    for load in loads:
        load.start()

    barrier = pltpu.get_barrier_semaphore()

    def lag_at(i):
        return lax.rem(my_lag + i, LAGS)

    def src_at(d):
        return lax.rem(my_src + d, SRCS)

    def greet(lag, src):
        pl.semaphore_signal(barrier, inc=1, device_id=(lag, src), device_id_type=MESH)

    def greet_group(d, carry):
        for i in range(LAGS):
            greet(lag_at(i), src_at(d))
        return carry

    for i in range(1, LAGS):
        greet(lag_at(i), my_src)
    lax.fori_loop(1, SRCS, greet_group, 0)
    pl.semaphore_wait(barrier, LAGS * SRCS - 1)

    s_f1, r_f1, s_f2, r_f2, s_f3, r_f3, s_r, s_m, r_m, s_p, s_c, r_c = [one_sem.at[i] for i in range(12)]
    own = plus.at[my_src, chip, core]
    for d in range(1, SRCS):
        remote(plus_ref, own, s_f1, r_f1, (my_lag, src_at(d)))
    pltpu.make_async_copy(plus_ref, own, r_f1).start()

    def send_reflection(lag, src):
        remote(refl_ref.at[src, lag], refl.at[my_src, my_lag], s_r, refl_sem.at[my_src], (lag, src))

    for i in range(1, LAGS):
        send_reflection(lag_at(i), my_src)
    pltpu.make_async_copy(refl_ref.at[my_src, my_lag], refl.at[my_src, my_lag], refl_sem.at[my_src]).start()

    column = plus.at[:, chip, core]
    wait(column, r_f1)
    for i in range(1, CHIPS):
        remote(column, column, s_f2, r_f2, (lag_at(2 * i), my_src))

    def send_group(d, carry):
        for i in range(LAGS):
            send_reflection(lag_at(i), src_at(d))
        return carry

    lax.fori_loop(1, SRCS, send_group, 0)
    wait(plus.at[:, pl.ds(0, CHIPS - 1), 0], r_f2)
    half = plus.at[:, :, core]
    other = chip * 2 + 1 - core
    remote(half, half, s_f3, r_f3, (other, my_src))
    for load in loads:
        load.wait()
    u_ref[...] = jnp.zeros_like(u_ref)
    wait(half, r_f3)

    def plus_spectra(g, carry):
        transform(lambda p: plus[g, p // 2, p % 2], a_ref, hf_ref.at[g], mats, turns)
        return carry

    lax.fori_loop(0, SRCS, plus_spectra, 0)

    def forward(d, carry):
        g = lax.rem(my_src + SRCS - d, SRCS)
        wait(refl.at[g], refl_sem.at[g])
        transform(lambda p: refl[g, p], a_ref, hr_ref.at[g], mats, turns)
        forward_terms(hr_ref.at[g], hf_ref.at[g], u_ref)
        return carry

    lax.fori_loop(0, SRCS, forward, 0)
    u_ref[...] = product(u_ref[...], mats, 1)
    middle(u_ref, b_ref, onset_r, RCV * my_lag, turns, minus)

    for i in range(1, LAGS):
        remote(minus.at[lag_at(i)], minus_out.at[my_lag], s_m, r_m, (lag_at(i), my_src))
    pltpu.make_async_copy(minus.at[my_lag], minus_out.at[my_lag], r_m).start()
    m_ref[...] = product(b_ref[...], mats, 0)

    def add_and_send(d):
        g = src_at(d)
        wait(peer.at[g], peer_sem.at[g])
        chip_sum[g] = (corr[g, core].astype(F32) + peer[g].astype(F32)).astype(BF16)
        for i in range(CHIPS):
            to = lax.rem(chip + i, CHIPS)
            remote(chip_sum.at[g, to], parts.at[my_src, chip], s_c, r_c, (to * 2 + core, g))

    def backward(d, carry):
        g = src_at(d)
        backward_terms(hr_ref.at[g], m_ref, c_ref)
        c_ref[...] = product(c_ref[...], mats, 2)
        kept = [load_blocks(turns, 2, c_ref, slice(8 * h, 8 * h + 8)) for h in range(2)]
        for p in range(BLOCKS):
            at = BLOCKS - 1 - p
            corr[g, p % 2, p // 2] = jnp.concatenate([kept[0][at], kept[1][at]], axis=0).astype(BF16)
        remote(corr.at[g, 1 - core], peer.at[g], s_p, peer_sem.at[g], (other, my_src))
        pl.when(d > 1)(lambda: add_and_send(d - 1))
        return carry

    lax.fori_loop(1, SRCS + 1, backward, 0)
    g = my_src
    wait(peer.at[g], peer_sem.at[g])
    chip_sum[g] = (corr[g, core].astype(F32) + peer[g].astype(F32)).astype(BF16)
    for i in range(1, CHIPS):
        to = lax.rem(chip + i, CHIPS)
        remote(chip_sum.at[g, to], parts.at[my_src, chip], s_c, r_c, (to * 2 + core, g))
    pltpu.make_async_copy(chip_sum.at[g, chip], parts.at[my_src, chip], r_c).start()

    lane = lax.broadcasted_iota(jnp.int32, (8, J), 1)
    masks = []
    for s in range(2):
        row = jnp.broadcast_to(onset_s[s : s + 1, :], (8, 8)).astype(F32)
        pick = lax.broadcasted_iota(jnp.int32, (8, 8), 0) == lax.broadcasted_iota(jnp.int32, (8, 8), 1)
        onset = jnp.sum(jnp.where(pick, row, 0.0), axis=1, keepdims=True)
        masks.append(window(jnp.broadcast_to(onset, (8, J)).astype(jnp.int32), lane + my_lag * J))
    wait(parts, r_c)
    total = jnp.zeros((16, J), F32)
    for g in range(SRCS):
        for l in range(CHIPS):
            total = total + parts[g, l].astype(F32)
    begin = start[...].astype(F32)
    for s in range(2):
        rows = slice(8 * s, 8 * s + 8)
        next_out[rows, :] = begin[rows] + jnp.where(masks[s], total[rows], 0.0)

    wait(minus_out, r_m)
    wait(plus.at[pl.ds(0, SRCS - 1), 0, 0], s_f1)
    wait(plus.at[:, pl.ds(0, CHIPS - 1), 0], s_f2)
    wait(half, s_f3)
    wait(refl.at[pl.ds(0, SRCS - 1)], s_r)
    wait(refl.at[0, pl.ds(0, LAGS - 1)], s_r)
    wait(minus_out.at[pl.ds(0, LAGS - 1)], s_m)
    wait(peer, s_p)
    wait(parts.at[pl.ds(0, SRCS - 1)], s_c)
    wait(parts.at[0, pl.ds(0, CHIPS - 1)], s_c)


def body(reflection, focus_plus, focus_start, onset_receiver, onset_source):
    anywhere = pl.BlockSpec(memory_space=pl.ANY)
    vmem = pl.BlockSpec(memory_space=pltpu.VMEM)
    matrices, turns = tables()
    spectra = pltpu.VMEM((SRCS, HALF, 16, 2 * J), F32)
    tiles = pltpu.VMEM((SRCS, CHIPS, 16, J), BF16)
    minus_out, next_out = pl.pallas_call(
        kernel,
        out_shape=(
            jax.ShapeDtypeStruct((LAGS, 8 * RCV, J), BF16),
            jax.ShapeDtypeStruct((16, J), F32),
        ),
        in_specs=[anywhere] * 7,
        out_specs=(vmem, vmem),
        scratch_shapes=[
            pltpu.VMEM((SRCS, LAGS, 16, J), BF16),
            pltpu.VMEM((SRCS, CHIPS, 2, 16, J), BF16),
            pltpu.VMEM(matrices.shape, BF16),
            pltpu.VMEM(turns.shape, F32),
            pltpu.VMEM((8, J), jnp.int32),
            pltpu.VMEM((2, 8), jnp.int32),
            pltpu.VMEM((16, J), BF16),
            pltpu.VMEM((HALF, 16, 2 * J), F32),
            spectra,
            spectra,
            pltpu.VMEM((HALF, 64, 2 * J), F32),
            pltpu.VMEM((HALF, 64, 2 * J), F32),
            pltpu.VMEM((HALF, 64, 2 * J), F32),
            pltpu.VMEM((HALF, 16, 2 * J), F32),
            pltpu.VMEM((LAGS, 8 * RCV, J), BF16),
            pltpu.VMEM((SRCS, 2, CHIPS, 16, J), BF16),
            tiles,
            tiles,
            tiles,
            pltpu.SemaphoreType.DMA((5,)),
            pltpu.SemaphoreType.DMA((12,)),
            pltpu.SemaphoreType.DMA((SRCS,)),
            pltpu.SemaphoreType.DMA((SRCS,)),
        ],
        compiler_params=pltpu.CompilerParams(
            collective_id=0, has_side_effects=True, vmem_limit_bytes=60 * 2**20
        ),
        name="focus",
    )(
        reflection.reshape(SRCS, LAGS, 16, J),
        focus_plus.reshape(16, J),
        focus_start.reshape(16, J),
        onset_receiver.T,
        onset_source,
        jnp.asarray(matrices),
        jnp.asarray(turns),
    )
    return minus_out.reshape(J, 8, J), next_out.reshape(2, 8, J)


def solution(mesh):
    return jax.shard_map(
        body,
        mesh=mesh,
        in_specs=(
            P(None, "src", "lag"),
            P("src", None, "lag"),
            P("src", None, "lag"),
            P(),
            P("src", None),
        ),
        out_specs=(P("src", None, "lag"), P("src", None, "lag")),
        check_vma=False,
    )
```

time: 75 us -> 48.6 us (0.65)
  Pallas kernels: 67.4 us -> 45.5 us
  local copies, waits for them, and re-layouts: 6.58 us -> 2.28 us
    pallas_call x3 -> x1, Pallas kernels: 67.4 us -> 45.5 us  [body(): pl.pallas_call(kernel, out_shape=(jax.ShapeDtypeStruct((LAGS, 8 * RCV, J)...]
    unnamed x16 -> x4, local copies, waits for them, and re-layouts: 6.13 us -> 2.28 us
where the time goes in v2:
time: 48.6 us; the launch traced here: 48.4 us
  Pallas kernels  45.5 us (94%)
  local copies, waits for them, and re-layouts  2.28 us (5%)
  between operations  0.65 us (1%)
    pallas_call x1, Pallas kernels, body(): pl.pallas_call(kernel, out_shape=(jax.ShapeDtypeStruct((LAGS, 8 * RCV, J)...  45.5 us
    unnamed x4, local copies, waits for them, and re-layouts  2.28 us

profile of v2, /device:TPU:1, one launch (start us, length us, event | category | flops | bytes accessed | tf_op | source)
XLA Modules:
  0.0 48.4 jit_solution(1377586890602324775)
XLA Ops:
  0.6 45.5 %focus.1 = (bf16[16,64,128]{2,1,0:T(8,128)(2,1)}, f32[16,128]{1,0:T(8,128)}) custom-call(bf16[8,16,16,128]{3,2,1,0:T(8,128)(2,1)} %bitcast.6, bf16[16,128]{1,0:T(8,128)(2,1)} %bitcast.10, bf16[16,128]{1,0:T(8,128)(2,1)} %bitcast.11, s32[8,1024]{1,0:T(8,128)} %bitcast.8, s32[2,8]{1,0:T(2,128)} %onset_s_ref.1, bf16[3,2,256,256]{3,2,1,0:T(8,128)(2,1)} %constant.4.clone.mat_hbm, ...), custom_call_target="tpu_custom_call" | custom-call | tf_op jit(solution)/shard_map/focus/pallas_call | solution.py:445
  46.1 0.0 copy-start
  46.1 1.7 %copy.11 = bf16[128,8,128]{2,1,0:T(8,128)(2,1)} copy(bf16[128,8,128]{2,1,0:T(8,128)(2,1)} %bitcast.7) | data formatting | bytes 524288
  47.8 0.0 copy-done
  47.8 0.6 %copy.12 = f32[2,8,128]{2,1,0:T(8,128)} copy(f32[2,8,128]{2,1,0:T(8,128)S(1)} %bitcast.9) | data formatting | bytes 16384
Async XLA Ops:
  46.1 1.7 %copy-start = (f32[16,128]{1,0:T(8,128)S(1)}, f32[16,128]{1,0:T(8,128)}, u32[]{:S(2)}) copy-start(f32[16,128]{1,0:T(8,128)} %get-tuple-element.5) | copy-start | bytes 24580

commit v3 on v2

--- a/solution.py
+++ b/solution.py
@@ -13,6 +13,8 @@
 LAGS, SRCS = 16, 8
 CHIPS = LAGS // 2
 RCV = 8
+EARLY = 5
+DEPTH = 2
 J = 128
 BLOCKS = 16
 RADIX = 32
@@ -280,7 +282,7 @@
     minus_out, next_out,
     refl, plus, mats, turns, onset_r, onset_s, start,
     a_ref, hr_ref, hf_ref, u_ref, b_ref, m_ref, c_ref,
-    minus, corr, peer, chip_sum, parts,
+    minus, corr, peer, chip_sum, parts, own_parts,
     local_sem, one_sem, refl_sem, peer_sem,
 ):
     my_lag, my_src = lax.axis_index("lag"), lax.axis_index("src")
@@ -323,41 +325,46 @@
     lax.fori_loop(1, SRCS, greet_group, 0)
     pl.semaphore_wait(barrier, LAGS * SRCS - 1)
 
-    s_f1, r_f1, s_f2, r_f2, s_f3, r_f3, s_r, s_m, r_m, s_p, s_c, r_c = [one_sem.at[i] for i in range(12)]
-    own = plus.at[my_src, chip, core]
-    for d in range(1, SRCS):
-        remote(plus_ref, own, s_f1, r_f1, (my_lag, src_at(d)))
-    pltpu.make_async_copy(plus_ref, own, r_f1).start()
+    s_f, r_f, s_f2, r_f2, s_r, s_m, r_m, s_p, s_c, r_c, s_o, r_o = [one_sem.at[i] for i in range(12)]
+
+    own = plus.at[core, my_src, chip]
+
+    def same_core(i):
+        return lax.rem(chip + i, CHIPS) * 2 + core
+
+    def send_plus(d, carry):
+        for i in range(CHIPS):
+            remote(plus_ref, own, s_f, r_f, (same_core(i), src_at(d)))
+        return carry
 
     def send_reflection(lag, src):
         remote(refl_ref.at[src, lag], refl.at[my_src, my_lag], s_r, refl_sem.at[my_src], (lag, src))
 
+    def send_group(d, carry):
+        for i in range(LAGS):
+            send_reflection(lag_at(i), src_at(d))
+        return carry
+
+    for i in range(1, CHIPS):
+        remote(plus_ref, own, s_f, r_f, (same_core(i), my_src))
+    pltpu.make_async_copy(plus_ref, own, r_f).start()
+    lax.fori_loop(1, SRCS, send_plus, 0)
     for i in range(1, LAGS):
         send_reflection(lag_at(i), my_src)
     pltpu.make_async_copy(refl_ref.at[my_src, my_lag], refl.at[my_src, my_lag], refl_sem.at[my_src]).start()
-
-    column = plus.at[:, chip, core]
-    wait(column, r_f1)
-    for i in range(1, CHIPS):
-        remote(column, column, s_f2, r_f2, (lag_at(2 * i), my_src))
-
-    def send_group(d, carry):
-        for i in range(LAGS):
-            send_reflection(lag_at(i), src_at(d))
-        return carry
-
-    lax.fori_loop(1, SRCS, send_group, 0)
-    wait(plus.at[:, pl.ds(0, CHIPS - 1), 0], r_f2)
-    half = plus.at[:, :, core]
+    lax.fori_loop(1, EARLY, send_group, 0)
+    half = plus.at[core]
     other = chip * 2 + 1 - core
-    remote(half, half, s_f3, r_f3, (other, my_src))
+    wait(half, r_f)
+    remote(half, half, s_f2, r_f2, (other, my_src))
+    lax.fori_loop(EARLY, SRCS, send_group, 0)
     for load in loads:
         load.wait()
     u_ref[...] = jnp.zeros_like(u_ref)
-    wait(half, r_f3)
+    wait(half, r_f2)
 
     def plus_spectra(g, carry):
-        transform(lambda p: plus[g, p // 2, p % 2], a_ref, hf_ref.at[g], mats, turns)
+        transform(lambda p: plus[p % 2, g, p // 2], a_ref, hf_ref.at[g], mats, turns)
         return carry
 
     lax.fori_loop(0, SRCS, plus_spectra, 0)
@@ -373,13 +380,20 @@
     u_ref[...] = product(u_ref[...], mats, 1)
     middle(u_ref, b_ref, onset_r, RCV * my_lag, turns, minus)
 
+    def send_minus(i):
+        remote(minus.at[lag_at(i)], minus_out.at[my_lag], s_m, r_m, (lag_at(i), my_src))
+
+    pltpu.make_async_copy(minus.at[my_lag], minus_out.at[my_lag], r_m).start()
     for i in range(1, LAGS):
-        remote(minus.at[lag_at(i)], minus_out.at[my_lag], s_m, r_m, (lag_at(i), my_src))
-    pltpu.make_async_copy(minus.at[my_lag], minus_out.at[my_lag], r_m).start()
+        send_minus(i)
     m_ref[...] = product(b_ref[...], mats, 0)
 
-    def add_and_send(d):
-        g = src_at(d)
+    def send_own():
+        for i in range(1, LAGS):
+            lag = lag_at(i)
+            remote(corr.at[my_src, lax.rem(lag, 2), lax.div(lag, 2)], own_parts.at[my_lag], s_o, r_o, (lag, my_src))
+
+    def add_and_send(g):
         wait(peer.at[g], peer_sem.at[g])
         chip_sum[g] = (corr[g, core].astype(F32) + peer[g].astype(F32)).astype(BF16)
         for i in range(CHIPS):
@@ -394,18 +408,19 @@
         for p in range(BLOCKS):
             at = BLOCKS - 1 - p
             corr[g, p % 2, p // 2] = jnp.concatenate([kept[0][at], kept[1][at]], axis=0).astype(BF16)
-        remote(corr.at[g, 1 - core], peer.at[g], s_p, peer_sem.at[g], (other, my_src))
-        pl.when(d > 1)(lambda: add_and_send(d - 1))
+
+        @pl.when(d < SRCS)
+        def _():
+            remote(corr.at[g, 1 - core], peer.at[g], s_p, peer_sem.at[g], (other, my_src))
+
+        pl.when(d == SRCS)(send_own)
+        pl.when(d > DEPTH)(lambda: add_and_send(src_at(d - DEPTH)))
         return carry
 
     lax.fori_loop(1, SRCS + 1, backward, 0)
-    g = my_src
-    wait(peer.at[g], peer_sem.at[g])
-    chip_sum[g] = (corr[g, core].astype(F32) + peer[g].astype(F32)).astype(BF16)
-    for i in range(1, CHIPS):
-        to = lax.rem(chip + i, CHIPS)
-        remote(chip_sum.at[g, to], parts.at[my_src, chip], s_c, r_c, (to * 2 + core, g))
-    pltpu.make_async_copy(chip_sum.at[g, chip], parts.at[my_src, chip], r_c).start()
+    for d in range(SRCS + 1 - DEPTH, SRCS):
+        add_and_send(src_at(d))
+    pltpu.make_async_copy(corr.at[my_src, core, chip], own_parts.at[my_lag], r_o).start()
 
     lane = lax.broadcasted_iota(jnp.int32, (8, J), 1)
     masks = []
@@ -414,30 +429,38 @@
         pick = lax.broadcasted_iota(jnp.int32, (8, 8), 0) == lax.broadcasted_iota(jnp.int32, (8, 8), 1)
         onset = jnp.sum(jnp.where(pick, row, 0.0), axis=1, keepdims=True)
         masks.append(window(jnp.broadcast_to(onset, (8, J)).astype(jnp.int32), lane + my_lag * J))
-    wait(parts, r_c)
-    total = jnp.zeros((16, J), F32)
-    for g in range(SRCS):
+    begin = start[...].astype(F32)
+    wait(parts.at[pl.ds(0, SRCS - 1)], r_c)
+    sums = [None] * 4
+    for d in range(1, SRCS):
         for l in range(CHIPS):
-            total = total + parts[g, l].astype(F32)
-    begin = start[...].astype(F32)
+            sums[l % 4] = add(sums[l % 4], parts[src_at(d), l].astype(F32))
+    wait(own_parts, r_o)
+    for l in range(LAGS):
+        sums[l % 4] = add(sums[l % 4], own_parts[l].astype(F32))
+    total = (sums[0] + sums[1]) + (sums[2] + sums[3])
     for s in range(2):
         rows = slice(8 * s, 8 * s + 8)
         next_out[rows, :] = begin[rows] + jnp.where(masks[s], total[rows], 0.0)
 
     wait(minus_out, r_m)
-    wait(plus.at[pl.ds(0, SRCS - 1), 0, 0], s_f1)
-    wait(plus.at[:, pl.ds(0, CHIPS - 1), 0], s_f2)
-    wait(half, s_f3)
+    wait(half.at[pl.ds(0, SRCS - 1)], s_f)
+    wait(half.at[0, pl.ds(0, CHIPS - 1)], s_f)
+    wait(half, s_f2)
     wait(refl.at[pl.ds(0, SRCS - 1)], s_r)
     wait(refl.at[0, pl.ds(0, LAGS - 1)], s_r)
     wait(minus_out.at[pl.ds(0, LAGS - 1)], s_m)
-    wait(peer, s_p)
+    wait(peer.at[pl.ds(0, SRCS - 1)], s_p)
     wait(parts.at[pl.ds(0, SRCS - 1)], s_c)
-    wait(parts.at[0, pl.ds(0, CHIPS - 1)], s_c)
+    wait(own_parts.at[pl.ds(0, LAGS - 1)], s_o)
+
+
+def finish_kernel(minus_ref, next_ref, minus_out, next_out):
+    minus_out[...] = minus_ref[...]
+    next_out[...] = next_ref[...]
 
 
 def body(reflection, focus_plus, focus_start, onset_receiver, onset_source):
-    anywhere = pl.BlockSpec(memory_space=pl.ANY)
     vmem = pl.BlockSpec(memory_space=pltpu.VMEM)
     matrices, turns = tables()
     spectra = pltpu.VMEM((SRCS, HALF, 16, 2 * J), F32)
@@ -448,11 +471,11 @@
             jax.ShapeDtypeStruct((LAGS, 8 * RCV, J), BF16),
             jax.ShapeDtypeStruct((16, J), F32),
         ),
-        in_specs=[anywhere] * 7,
+        in_specs=[pl.BlockSpec(memory_space=pl.ANY)] * 7,
         out_specs=(vmem, vmem),
         scratch_shapes=[
             pltpu.VMEM((SRCS, LAGS, 16, J), BF16),
-            pltpu.VMEM((SRCS, CHIPS, 2, 16, J), BF16),
+            pltpu.VMEM((2, SRCS, CHIPS, 16, J), BF16),
             pltpu.VMEM(matrices.shape, BF16),
             pltpu.VMEM(turns.shape, F32),
             pltpu.VMEM((8, J), jnp.int32),
@@ -470,6 +493,7 @@
             tiles,
             tiles,
             tiles,
+            pltpu.VMEM((LAGS, 16, J), BF16),
             pltpu.SemaphoreType.DMA((5,)),
             pltpu.SemaphoreType.DMA((12,)),
             pltpu.SemaphoreType.DMA((SRCS,)),
@@ -488,6 +512,16 @@
         jnp.asarray(matrices),
         jnp.asarray(turns),
     )
+    minus_out, next_out = pl.pallas_call(
+        finish_kernel,
+        out_shape=(
+            jax.ShapeDtypeStruct(minus_out.shape, BF16),
+            jax.ShapeDtypeStruct(next_out.shape, F32),
+        ),
+        in_specs=[vmem] * 2,
+        out_specs=(vmem, vmem),
+        name="finish",
+    )(minus_out, next_out)
     return minus_out.reshape(J, 8, J), next_out.reshape(2, 8, J)
 
 

time: 48.6 us -> 43.8 us (0.901)
  Pallas kernels: 45.5 us -> 43.1 us
  local copies, waits for them, and re-layouts: 2.28 us -> 0 us
    pallas_call x1, Pallas kernels: 45.5 us -> 41.4 us  [body(): pl.pallas_call(kernel, out_shape=(jax.ShapeDtypeStruct((LAGS, 8 * RCV, J)...]
    unnamed x4 -> x0, local copies, waits for them, and re-layouts: 2.28 us -> none
    pallas_call x0 -> x1, Pallas kernels: none -> 1.68 us  [body(): pl.pallas_call(finish_kernel, out_shape=(jax.ShapeDtypeStruct(minus_out.s...]
where the time goes in v3:
time: 43.8 us; the launch traced here: 43.7 us
  Pallas kernels  43.1 us (98%)
  between operations  0.64 us (1%)
    pallas_call x1, Pallas kernels, body(): pl.pallas_call(kernel, out_shape=(jax.ShapeDtypeStruct((LAGS, 8 * RCV, J)...  41.4 us
    pallas_call x1, Pallas kernels, body(): pl.pallas_call(finish_kernel, out_shape=(jax.ShapeDtypeStruct(minus_out.s...  1.68 us

profile of v3, /device:TPU:1, one launch (start us, length us, event | category | flops | bytes accessed | tf_op | source)
XLA Modules:
  0.0 43.7 jit_solution(12033889567590266418)
XLA Ops:
  0.6 41.4 %focus.1 = (bf16[16,64,128]{2,1,0:T(8,128)(2,1)}, f32[16,128]{1,0:T(8,128)}) custom-call(bf16[8,16,16,128]{3,2,1,0:T(8,128)(2,1)} %bitcast.6, bf16[16,128]{1,0:T(8,128)(2,1)} %bitcast.8, bf16[16,128]{1,0:T(8,128)(2,1)} %bitcast.9, s32[8,1024]{1,0:T(8,128)} %bitcast.7, s32[2,8]{1,0:T(2,128)} %onset_s_ref.1, bf16[3,2,256,256]{3,2,1,0:T(8,128)(2,1)} %constant.4.clone.mat_hbm, ...), custom_call_target="tpu_custom_call" | custom-call | tf_op jit(solution)/shard_map/focus/pallas_call | solution.py:468
  42.0 1.7 %finish.1 = (bf16[16,64,128]{2,1,0:T(8,128)(2,1)}, f32[16,128]{1,0:T(8,128)}) custom-call(bf16[16,64,128]{2,1,0:T(8,128)(2,1)} %get-tuple-element.6.minus_ref, f32[16,128]{1,0:T(8,128)} %get-tuple-element.7.next_ref), custom_call_target="tpu_custom_call" | custom-call | tf_op jit(solution)/shard_map/finish/pallas_call | solution.py:515

commit v4 on v3

--- a/solution.py
+++ b/solution.py
@@ -15,6 +15,7 @@
 RCV = 8
 EARLY = 5
 DEPTH = 2
+AHEAD = 2
 J = 128
 BLOCKS = 16
 RADIX = 32
@@ -200,12 +201,19 @@
     return out.reshape(shape)
 
 
-def transform(tile, a_ref, out_ref, mat_ref, turn_ref):
+def first_part(tile, a_ref, turn_ref):
     values = [tile(p).astype(F32) for p in range(BLOCKS)]
     for half in range(2):
         rows = slice(8 * half, 8 * half + 8)
         store_spectrum(turn_ref, [v[rows] for v in values], a_ref, rows)
-    out_ref[...] = product(a_ref[...], mat_ref, 0)
+
+
+def transform(tiles, a_ref, outs, mat_ref, turn_ref):
+    for i, tile in enumerate(tiles):
+        first_part(tile, a_ref.at[pl.ds(i * HALF, HALF)], turn_ref)
+    result = product(a_ref[0 : len(tiles) * HALF], mat_ref, 0)
+    for i, out in enumerate(outs):
+        out[...] = result[i * HALF : (i + 1) * HALF]
 
 
 def both(ref, k, row):
@@ -278,11 +286,11 @@
 
 
 def kernel(
-    refl_ref, plus_ref, start_ref, onset_r_ref, onset_s_ref, mat_hbm, turn_hbm,
-    minus_out, next_out,
-    refl, plus, mats, turns, onset_r, onset_s, start,
+    refl_ref, plus_ref, onset_r_ref, mat_hbm, turn_hbm,
+    minus_out, parts, own_parts,
+    refl, plus, mats, turns, onset_r,
     a_ref, hr_ref, hf_ref, u_ref, b_ref, m_ref, c_ref,
-    minus, corr, peer, chip_sum, parts, own_parts,
+    minus, corr, peer, chip_sum,
     local_sem, one_sem, refl_sem, peer_sem,
 ):
     my_lag, my_src = lax.axis_index("lag"), lax.axis_index("src")
@@ -297,7 +305,7 @@
         pltpu.make_async_copy(ref, ref, sem).wait()
 
     loads = [
-        (mat_hbm, mats), (turn_hbm, turns), (start_ref, start), (onset_s_ref, onset_s),
+        (mat_hbm, mats), (turn_hbm, turns),
         (onset_r_ref.at[:, pl.ds(pl.multiple_of(my_src * J, J), J)], onset_r),
     ]
     loads = [pltpu.make_async_copy(a, b, local_sem.at[i]) for i, (a, b) in enumerate(loads)]
@@ -361,18 +369,33 @@
     for load in loads:
         load.wait()
     u_ref[...] = jnp.zeros_like(u_ref)
+
+    def source(d):
+        return lax.rem(my_src + SRCS - d, SRCS)
+
+    def reflection_spectra(groups):
+        for g in groups:
+            wait(refl.at[g], refl_sem.at[g])
+        tiles = [lambda p, g=g: refl[g, p] for g in groups]
+        transform(tiles, a_ref, [hr_ref.at[g] for g in groups], mats, turns)
+
+    def early(i, carry):
+        reflection_spectra([source(2 * i), source(2 * i + 1)])
+        return carry
+
+    lax.fori_loop(0, AHEAD // 2, early, 0)
     wait(half, r_f2)
 
-    def plus_spectra(g, carry):
-        transform(lambda p: plus[p % 2, g, p // 2], a_ref, hf_ref.at[g], mats, turns)
-        return carry
-
-    lax.fori_loop(0, SRCS, plus_spectra, 0)
+    def plus_spectra(i, carry):
+        tiles = [lambda p, g=g: plus[p % 2, g, p // 2] for g in (2 * i, 2 * i + 1)]
+        transform(tiles, a_ref, [hf_ref.at[2 * i], hf_ref.at[2 * i + 1]], mats, turns)
+        return carry
+
+    lax.fori_loop(0, SRCS // 2, plus_spectra, 0)
 
     def forward(d, carry):
-        g = lax.rem(my_src + SRCS - d, SRCS)
-        wait(refl.at[g], refl_sem.at[g])
-        transform(lambda p: refl[g, p], a_ref, hr_ref.at[g], mats, turns)
+        g = source(d)
+        pl.when(d >= AHEAD)(lambda: reflection_spectra([g]))
         forward_terms(hr_ref.at[g], hf_ref.at[g], u_ref)
         return carry
 
@@ -422,27 +445,8 @@
         add_and_send(src_at(d))
     pltpu.make_async_copy(corr.at[my_src, core, chip], own_parts.at[my_lag], r_o).start()
 
-    lane = lax.broadcasted_iota(jnp.int32, (8, J), 1)
-    masks = []
-    for s in range(2):
-        row = jnp.broadcast_to(onset_s[s : s + 1, :], (8, 8)).astype(F32)
-        pick = lax.broadcasted_iota(jnp.int32, (8, 8), 0) == lax.broadcasted_iota(jnp.int32, (8, 8), 1)
-        onset = jnp.sum(jnp.where(pick, row, 0.0), axis=1, keepdims=True)
-        masks.append(window(jnp.broadcast_to(onset, (8, J)).astype(jnp.int32), lane + my_lag * J))
-    begin = start[...].astype(F32)
     wait(parts.at[pl.ds(0, SRCS - 1)], r_c)
-    sums = [None] * 4
-    for d in range(1, SRCS):
-        for l in range(CHIPS):
-            sums[l % 4] = add(sums[l % 4], parts[src_at(d), l].astype(F32))
     wait(own_parts, r_o)
-    for l in range(LAGS):
-        sums[l % 4] = add(sums[l % 4], own_parts[l].astype(F32))
-    total = (sums[0] + sums[1]) + (sums[2] + sums[3])
-    for s in range(2):
-        rows = slice(8 * s, 8 * s + 8)
-        next_out[rows, :] = begin[rows] + jnp.where(masks[s], total[rows], 0.0)
-
     wait(minus_out, r_m)
     wait(half.at[pl.ds(0, SRCS - 1)], s_f)
     wait(half.at[0, pl.ds(0, CHIPS - 1)], s_f)
@@ -455,9 +459,26 @@
     wait(own_parts.at[pl.ds(0, LAGS - 1)], s_o)
 
 
-def finish_kernel(minus_ref, next_ref, minus_out, next_out):
+def finish_kernel(minus_ref, parts, own_parts, start, onset_s, minus_out, next_out):
+    my_lag, my_src = lax.axis_index("lag"), lax.axis_index("src")
     minus_out[...] = minus_ref[...]
-    next_out[...] = next_ref[...]
+    lane = lax.broadcasted_iota(jnp.int32, (8, J), 1)
+    sums = [own_parts[l].astype(F32) for l in range(4)]
+    for l in range(4, LAGS):
+        sums[l % 4] = sums[l % 4] + own_parts[l].astype(F32)
+    for d in range(1, SRCS):
+        g = lax.rem(my_src + d, SRCS)
+        for l in range(CHIPS):
+            sums[l % 4] = sums[l % 4] + parts[g, l].astype(F32)
+    total = (sums[0] + sums[1]) + (sums[2] + sums[3])
+    begin = start[...].astype(F32)
+    for s in range(2):
+        row = jnp.broadcast_to(onset_s[s : s + 1, :], (8, 8)).astype(F32)
+        pick = lax.broadcasted_iota(jnp.int32, (8, 8), 0) == lax.broadcasted_iota(jnp.int32, (8, 8), 1)
+        onset = jnp.sum(jnp.where(pick, row, 0.0), axis=1, keepdims=True)
+        mask = window(jnp.broadcast_to(onset, (8, J)).astype(jnp.int32), lane + my_lag * J)
+        rows = slice(8 * s, 8 * s + 8)
+        next_out[rows, :] = begin[rows] + jnp.where(mask, total[rows], 0.0)
 
 
 def body(reflection, focus_plus, focus_start, onset_receiver, onset_source):
@@ -465,23 +486,22 @@
     matrices, turns = tables()
     spectra = pltpu.VMEM((SRCS, HALF, 16, 2 * J), F32)
     tiles = pltpu.VMEM((SRCS, CHIPS, 16, J), BF16)
-    minus_out, next_out = pl.pallas_call(
+    minus_out, parts, own_parts = pl.pallas_call(
         kernel,
         out_shape=(
             jax.ShapeDtypeStruct((LAGS, 8 * RCV, J), BF16),
-            jax.ShapeDtypeStruct((16, J), F32),
+            jax.ShapeDtypeStruct((SRCS, CHIPS, 16, J), BF16),
+            jax.ShapeDtypeStruct((LAGS, 16, J), BF16),
         ),
-        in_specs=[pl.BlockSpec(memory_space=pl.ANY)] * 7,
-        out_specs=(vmem, vmem),
+        in_specs=[pl.BlockSpec(memory_space=pl.ANY)] * 5,
+        out_specs=(pl.BlockSpec(memory_space=pl.ANY),) * 3,
         scratch_shapes=[
             pltpu.VMEM((SRCS, LAGS, 16, J), BF16),
             pltpu.VMEM((2, SRCS, CHIPS, 16, J), BF16),
             pltpu.VMEM(matrices.shape, BF16),
             pltpu.VMEM(turns.shape, F32),
             pltpu.VMEM((8, J), jnp.int32),
-            pltpu.VMEM((2, 8), jnp.int32),
-            pltpu.VMEM((16, J), BF16),
-            pltpu.VMEM((HALF, 16, 2 * J), F32),
+            pltpu.VMEM((2 * HALF, 16, 2 * J), F32),
             spectra,
             spectra,
             pltpu.VMEM((HALF, 64, 2 * J), F32),
@@ -492,9 +512,7 @@
             pltpu.VMEM((SRCS, 2, CHIPS, 16, J), BF16),
             tiles,
             tiles,
-            tiles,
-            pltpu.VMEM((LAGS, 16, J), BF16),
-            pltpu.SemaphoreType.DMA((5,)),
+            pltpu.SemaphoreType.DMA((3,)),
             pltpu.SemaphoreType.DMA((12,)),
             pltpu.SemaphoreType.DMA((SRCS,)),
             pltpu.SemaphoreType.DMA((SRCS,)),
@@ -506,9 +524,7 @@
     )(
         reflection.reshape(SRCS, LAGS, 16, J),
         focus_plus.reshape(16, J),
-        focus_start.reshape(16, J),
         onset_receiver.T,
-        onset_source,
         jnp.asarray(matrices),
         jnp.asarray(turns),
     )
@@ -516,12 +532,12 @@
         finish_kernel,
         out_shape=(
             jax.ShapeDtypeStruct(minus_out.shape, BF16),
-            jax.ShapeDtypeStruct(next_out.shape, F32),
+            jax.ShapeDtypeStruct((16, J), F32),
         ),
-        in_specs=[vmem] * 2,
+        in_specs=[vmem] * 5,
         out_specs=(vmem, vmem),
         name="finish",
-    )(minus_out, next_out)
+    )(minus_out, parts, own_parts, focus_start.reshape(16, J), onset_source)
     return minus_out.reshape(J, 8, J), next_out.reshape(2, 8, J)
 
 

time: 43.8 us -> 42.7 us (0.975)
  Pallas kernels: 43.1 us -> 41.9 us
    pallas_call x1, Pallas kernels: 41.4 us -> 40.1 us  [body(): pl.pallas_call(kernel, out_shape=(jax.ShapeDtypeStruct((LAGS, 8 * RCV, J)...]
where the time goes in v4:
time: 42.7 us; the launch traced here: 42.5 us
  Pallas kernels  41.9 us (98%)
  between operations  0.64 us (1%)
    pallas_call x1, Pallas kernels, body(): pl.pallas_call(kernel, out_shape=(jax.ShapeDtypeStruct((LAGS, 8 * RCV, J)...  40.1 us
    pallas_call x1, Pallas kernels, body(): pl.pallas_call(finish_kernel, out_shape=(jax.ShapeDtypeStruct(minus_out.s...  1.78 us

profile of v4, /device:TPU:1, one launch (start us, length us, event | category | flops | bytes accessed | tf_op | source)
XLA Modules:
  0.0 42.5 jit_solution(645761865129198)
XLA Ops:
  0.6 40.1 %focus.1 = (bf16[16,64,128]{2,1,0:T(8,128)(2,1)}, bf16[8,8,16,128]{3,2,1,0:T(8,128)(2,1)}, bf16[16,16,128]{2,1,0:T(8,128)(2,1)}) custom-call(bf16[8,16,16,128]{3,2,1,0:T(8,128)(2,1)} %bitcast.6, bf16[16,128]{1,0:T(8,128)(2,1)} %bitcast.8, s32[8,1024]{1,0:T(8,128)} %bitcast.7, bf16[3,2,256,256]{3,2,1,0:T(8,128)(2,1)} %constant.4.clone.mat_hbm, ...), custom_call_target="tpu_custom_call" | custom-call | tf_op jit(solution)/shard_map/focus/pallas_call | solution.py:489
  40.8 1.8 %finish.1 = (bf16[16,64,128]{2,1,0:T(8,128)(2,1)}, f32[16,128]{1,0:T(8,128)}) custom-call(bf16[16,64,128]{2,1,0:T(8,128)(2,1)} %get-tuple-element.7.minus_ref, bf16[8,8,16,128]{3,2,1,0:T(8,128)(2,1)} %get-tuple-element.8.parts, bf16[16,16,128]{2,1,0:T(8,128)(2,1)} %get-tuple-element.9.own_parts, bf16[16,128]{1,0:T(8,128)(2,1)} %bitcast.9, s32[2,8]{1,0:T(2,128)} %onset_s.1), custom_call_target="tpu_custom_call" | custom-call | tf_op jit(solution)/shard_map/finish/pallas_call | solution.py:531

commit v5 on v4

--- a/solution.py
+++ b/solution.py
@@ -13,8 +13,7 @@
 LAGS, SRCS = 16, 8
 CHIPS = LAGS // 2
 RCV = 8
-EARLY = 5
-DEPTH = 2
+EARLY = 7
 AHEAD = 2
 J = 128
 BLOCKS = 16
@@ -423,26 +422,42 @@
             to = lax.rem(chip + i, CHIPS)
             remote(chip_sum.at[g, to], parts.at[my_src, chip], s_c, r_c, (to * 2 + core, g))
 
-    def backward(d, carry):
-        g = src_at(d)
-        backward_terms(hr_ref.at[g], m_ref, c_ref)
-        c_ref[...] = product(c_ref[...], mats, 2)
-        kept = [load_blocks(turns, 2, c_ref, slice(8 * h, 8 * h + 8)) for h in range(2)]
-        for p in range(BLOCKS):
-            at = BLOCKS - 1 - p
-            corr[g, p % 2, p // 2] = jnp.concatenate([kept[0][at], kept[1][at]], axis=0).astype(BF16)
-
-        @pl.when(d < SRCS)
+    def partial_sums(groups):
+        for h, g in enumerate(groups):
+            backward_terms(hr_ref.at[g], m_ref, c_ref.at[pl.ds(h * HALF, HALF)])
+        filled = slice(0, len(groups) * HALF)
+        c_ref[filled] = product(c_ref[filled], mats, 2)
+        for h, g in enumerate(groups):
+            c_part = c_ref.at[pl.ds(h * HALF, HALF)]
+            kept = [load_blocks(turns, 2, c_part, slice(8 * s, 8 * s + 8)) for s in range(2)]
+            for p in range(BLOCKS):
+                at = BLOCKS - 1 - p
+                corr[g, p % 2, p // 2] = jnp.concatenate([kept[0][at], kept[1][at]], axis=0).astype(BF16)
+
+    def to_other_core(g):
+        remote(corr.at[g, 1 - core], peer.at[g], s_p, peer_sem.at[g], (other, my_src))
+
+    def backward(i, carry):
+        groups = [src_at(2 * i + 1), src_at(2 * i + 2)]
+        partial_sums(groups)
+        for g in groups:
+            to_other_core(g)
+
+        @pl.when(i > 0)
         def _():
-            remote(corr.at[g, 1 - core], peer.at[g], s_p, peer_sem.at[g], (other, my_src))
-
-        pl.when(d == SRCS)(send_own)
-        pl.when(d > DEPTH)(lambda: add_and_send(src_at(d - DEPTH)))
-        return carry
-
-    lax.fori_loop(1, SRCS + 1, backward, 0)
-    for d in range(SRCS + 1 - DEPTH, SRCS):
-        add_and_send(src_at(d))
+            add_and_send(src_at(2 * i - 1))
+            add_and_send(src_at(2 * i))
+
+        return carry
+
+    lax.fori_loop(0, SRCS // 2 - 1, backward, 0)
+    partial_sums([src_at(SRCS - 1)])
+    to_other_core(src_at(SRCS - 1))
+    add_and_send(src_at(SRCS - 3))
+    add_and_send(src_at(SRCS - 2))
+    partial_sums([my_src])
+    send_own()
+    add_and_send(src_at(SRCS - 1))
     pltpu.make_async_copy(corr.at[my_src, core, chip], own_parts.at[my_lag], r_o).start()
 
     wait(parts.at[pl.ds(0, SRCS - 1)], r_c)
@@ -507,7 +522,7 @@
             pltpu.VMEM((HALF, 64, 2 * J), F32),
             pltpu.VMEM((HALF, 64, 2 * J), F32),
             pltpu.VMEM((HALF, 64, 2 * J), F32),
-            pltpu.VMEM((HALF, 16, 2 * J), F32),
+            pltpu.VMEM((2 * HALF, 16, 2 * J), F32),
             pltpu.VMEM((LAGS, 8 * RCV, J), BF16),
             pltpu.VMEM((SRCS, 2, CHIPS, 16, J), BF16),
             tiles,

time: 42.7 us -> 42 us (0.984)
  Pallas kernels: 41.9 us -> 41.2 us
    pallas_call x1, Pallas kernels: 40.1 us -> 39.5 us  [body(): pl.pallas_call(kernel, out_shape=(jax.ShapeDtypeStruct((LAGS, 8 * RCV, J)...]
where the time goes in v5:
time: 42 us; the launch traced here: 41.9 us
  Pallas kernels  41.2 us (98%)
  between operations  0.64 us (2%)
    pallas_call x1, Pallas kernels, body(): pl.pallas_call(kernel, out_shape=(jax.ShapeDtypeStruct((LAGS, 8 * RCV, J)...  39.5 us
    pallas_call x1, Pallas kernels, body(): pl.pallas_call(finish_kernel, out_shape=(jax.ShapeDtypeStruct(minus_out.s...  1.78 us

profile of v5, /device:TPU:1, one launch (start us, length us, event | category | flops | bytes accessed | tf_op | source)
XLA Modules:
  0.0 41.9 jit_solution(4472335481787411029)
XLA Ops:
  0.6 39.5 %focus.1 = (bf16[16,64,128]{2,1,0:T(8,128)(2,1)}, bf16[8,8,16,128]{3,2,1,0:T(8,128)(2,1)}, bf16[16,16,128]{2,1,0:T(8,128)(2,1)}) custom-call(bf16[8,16,16,128]{3,2,1,0:T(8,128)(2,1)} %bitcast.6, bf16[16,128]{1,0:T(8,128)(2,1)} %bitcast.8, s32[8,1024]{1,0:T(8,128)} %bitcast.7, bf16[3,2,256,256]{3,2,1,0:T(8,128)(2,1)} %constant.4.clone.mat_hbm, ...), custom_call_target="tpu_custom_call" | custom-call | tf_op jit(solution)/shard_map/focus/pallas_call | solution.py:504
  40.1 1.8 %finish.1 = (bf16[16,64,128]{2,1,0:T(8,128)(2,1)}, f32[16,128]{1,0:T(8,128)}) custom-call(bf16[16,64,128]{2,1,0:T(8,128)(2,1)} %get-tuple-element.7.minus_ref, bf16[8,8,16,128]{3,2,1,0:T(8,128)(2,1)} %get-tuple-element.8.parts, bf16[16,16,128]{2,1,0:T(8,128)(2,1)} %get-tuple-element.9.own_parts, bf16[16,128]{1,0:T(8,128)(2,1)} %bitcast.9, s32[2,8]{1,0:T(2,128)} %onset_s.1), custom_call_target="tpu_custom_call" | custom-call | tf_op jit(solution)/shard_map/finish/pallas_call | solution.py:546

commit v6 on v5

--- a/solution.py
+++ b/solution.py
@@ -13,7 +13,7 @@
 LAGS, SRCS = 16, 8
 CHIPS = LAGS // 2
 RCV = 8
-EARLY = 7
+EARLY = 8
 AHEAD = 2
 J = 128
 BLOCKS = 16

time: 42 us -> 42 us (level)
  no operation moved by 1% of the time
where the time goes in v6:
time: 42 us; the launch traced here: 41.9 us
  Pallas kernels  41.2 us (98%)
  between operations  0.64 us (2%)
    pallas_call x1, Pallas kernels, body(): pl.pallas_call(kernel, out_shape=(jax.ShapeDtypeStruct((LAGS, 8 * RCV, J)...  39.5 us
    pallas_call x1, Pallas kernels, body(): pl.pallas_call(finish_kernel, out_shape=(jax.ShapeDtypeStruct(minus_out.s...  1.78 us

profile of v6, /device:TPU:1, one launch (start us, length us, event | category | flops | bytes accessed | tf_op | source)
XLA Modules:
  0.0 41.9 jit_solution(12413880903311869588)
XLA Ops:
  0.6 39.5 %focus.1 = (bf16[16,64,128]{2,1,0:T(8,128)(2,1)}, bf16[8,8,16,128]{3,2,1,0:T(8,128)(2,1)}, bf16[16,16,128]{2,1,0:T(8,128)(2,1)}) custom-call(bf16[8,16,16,128]{3,2,1,0:T(8,128)(2,1)} %bitcast.6, bf16[16,128]{1,0:T(8,128)(2,1)} %bitcast.8, s32[8,1024]{1,0:T(8,128)} %bitcast.7, bf16[3,2,256,256]{3,2,1,0:T(8,128)(2,1)} %constant.4.clone.mat_hbm, ...), custom_call_target="tpu_custom_call" | custom-call | tf_op jit(solution)/shard_map/focus/pallas_call | solution.py:504
  40.1 1.8 %finish.1 = (bf16[16,64,128]{2,1,0:T(8,128)(2,1)}, f32[16,128]{1,0:T(8,128)}) custom-call(bf16[16,64,128]{2,1,0:T(8,128)(2,1)} %get-tuple-element.7.minus_ref, bf16[8,8,16,128]{3,2,1,0:T(8,128)(2,1)} %get-tuple-element.8.parts, bf16[16,16,128]{2,1,0:T(8,128)(2,1)} %get-tuple-element.9.own_parts, bf16[16,128]{1,0:T(8,128)(2,1)} %bitcast.9, s32[2,8]{1,0:T(2,128)} %onset_s.1), custom_call_target="tpu_custom_call" | custom-call | tf_op jit(solution)/shard_map/finish/pallas_call | solution.py:546
